TPU v7x, 32 devices: a whole 2x2x4 slice. The times are simulated.
32 devices in a mesh: dp: 4 (over x, core), ctx: 2 (over y), tensor: 4 (over z).
Axes of the slice: x: 2, y: 2, z: 4, core: 2. Of those that a mesh axis runs over, the one named last changes fastest.
Arguments:
- block_input: bfloat16 [4, 4096, 768], P('dp', 'ctx'), may hold values from -6 to 6
- cotangent: bfloat16 [4, 4096, 768], P('dp', 'ctx'), may hold values from -6 to 6
- norm1_gain: bfloat16 [768], P('dp'), may hold values from 0.25 to 1.75
- norm1_bias: bfloat16 [768], P('dp'), may hold values from -1.5 to 1.5
- qkv_weight: bfloat16 [768, 3, 768], P('dp', None, 'tensor'), may hold values from -0.21875 to 0.21875
- qkv_bias: bfloat16 [2, 12, 64], P(None, 'tensor', 'dp'), may hold values from -1.5 to 1.5
- rel_pos_h: bfloat16 [127, 64], P(None, 'dp'), may hold values from -0.75 to 0.75
- rel_pos_w: bfloat16 [127, 64], P(None, 'dp'), may hold values from -0.75 to 0.75
- proj_weight: bfloat16 [768, 768], P('tensor', 'dp'), may hold values from -3 to 3
- proj_bias: bfloat16 [768], P('dp'), may hold values from -1.5 to 1.5
- norm2_gain: bfloat16 [768], P('dp'), may hold values from 0.25 to 1.75
- norm2_bias: bfloat16 [768], P('dp'), may hold values from -1.5 to 1.5
- mlp_in_weight: bfloat16 [768, 3072], P('dp', 'tensor'), may hold values from -0.21875 to 0.21875
- mlp_in_bias: bfloat16 [48, 64], P('tensor', 'dp'), may hold values from -2 to 2
- mlp_out_weight: bfloat16 [3072, 768], P('tensor', 'dp'), may hold values from -0.15625 to 0.15625
- mlp_out_bias: bfloat16 [768], P('dp'), may hold values from -1.5 to 1.5
Outputs:
- block_out: bfloat16 [4, 4096, 768], P('dp', 'ctx')
- grad_input: float32 [4, 4096, 768], P('dp', 'ctx')
- grad_norm1_gain: float32 [768], P('dp')
- grad_norm1_bias: float32 [768], P('dp')
- grad_qkv_weight: float32 [768, 3, 768], P('dp', None, 'tensor')
- grad_qkv_bias: float32 [2, 12, 64], P(None, 'tensor', 'dp')
- grad_rel_pos_h: float32 [127, 64], P(None, 'dp')
- grad_rel_pos_w: float32 [127, 64], P(None, 'dp')
- grad_proj_weight: float32 [768, 768], P('tensor', 'dp')
- grad_proj_bias: float32 [768], P('dp')
- grad_norm2_gain: float32 [768], P('dp')
- grad_norm2_bias: float32 [768], P('dp')
- grad_mlp_in_weight: float32 [768, 3072], P('dp', 'tensor')
- grad_mlp_in_bias: float32 [48, 64], P('tensor', 'dp')
- grad_mlp_out_weight: float32 [3072, 768], P('tensor', 'dp')
- grad_mlp_out_bias: float32 [768], P('dp')
All inputs are finite; a program needn't handle non-finite values.
Results may differ from a plain program's by a relative error of at most 0.023.
Values may be sent and summed in bfloat16 or wider, within the bound.
No kernel may reach another device: no remote copies, remote signals or barrier semaphores. Data moves between devices by JAX's collectives and lax.ppermute only.
A program may use at most 384 MiB of HBM per device.

v0:
```python
import functools

import jax
import jax.numpy as jnp
from jax import lax
from jax.experimental import pallas as pl
from jax.experimental.pallas import tpu as pltpu
from jax.sharding import PartitionSpec as P

HD = 64
GW = 64
EPS = 1e-06
f32 = jnp.float32
bf16 = jnp.bfloat16
VMEM = 56 * 2**20


def iota(shape, dim):
    return lax.broadcasted_iota(jnp.int32, shape, dim)


def dot(a, b, ca, cb):
    return lax.dot_general(a, b, (((ca,), (cb,)), ((), ())), preferred_element_type=f32)


def make_qaug(qT, tab, il0, off, R):
    bq = qT.shape[1]
    qf = jnp.concatenate([qT.astype(f32), jnp.zeros((64, bq), f32)], 0).T
    g = dot(qT, tab, 0, 0)
    lane = iota((64, 128), 1)
    used = (lane < 64 + R) | ((lane >= 96) & (lane < 96 + R))
    outs = []
    for k in range(bq // 64):
        gh = g[k * 64 : (k + 1) * 64, :128]
        gw = g[k * 64 : (k + 1) * 64, 128:]
        sh = 63 - (il0 + k) + off
        h64 = pltpu.roll(gh, lax.rem(64 - sh + 256, 128), 1)
        h96 = pltpu.roll(gh, lax.rem(96 - sh + 256, 128), 1)
        w64 = pltpu.roll(gw, 1, 1, stride=1, stride_axis=0)
        w0 = pltpu.roll(gw, 65, 1, stride=1, stride_axis=0)
        a = jnp.where(lane < 64, qf[k * 64 : (k + 1) * 64], w64)
        wl = w0 - w0.astype(bf16).astype(f32)
        hl = h96 - h96.astype(bf16).astype(f32)
        b = jnp.where(lane < 64, wl, jnp.where(lane < 96, h64, hl))
        b = jnp.where(used, b, 0.0)
        outs.append(jnp.concatenate([a, b], 1).astype(bf16))
    return jnp.concatenate(outs, 0)


def build_kaug(kT, kaug, flipped=False):
    KB = kT.shape[1]
    ck = min(512, KB)
    for c in range(KB // ck):
        kf = kT[:, c * ck : (c + 1) * ck].astype(f32) * 0.125
        kf = jnp.concatenate([kf, jnp.zeros((64, ck), f32)], 0).T
        n = iota((ck, 128), 0) + c * ck
        lane = iota((ck, 128), 1)
        col, row = n & 63, n >> 6
        spot = 127 - col if flipped else 64 + col
        a = jnp.where(lane < 64, kf, (lane == spot).astype(f32))
        b = jnp.where(lane < 64, (lane == col).astype(f32), ((lane & 31) == row).astype(f32))
        kaug[c * ck : (c + 1) * ck, :] = jnp.concatenate([a, b], 1).astype(bf16)


def build_kaugT(kT, kaugT):
    KB = kT.shape[1]
    ck = min(512, KB)
    for c in range(KB // ck):
        f = iota((64, ck), 0)
        n = iota((64, ck), 1) + c * ck
        col, row = n & 63, n >> 6
        sl = slice(c * ck, (c + 1) * ck)
        kaugT[0:64, sl] = (kT[:, sl].astype(f32) * 0.125).astype(bf16)
        oc = (f == col).astype(f32).astype(bf16)
        kaugT[64:128, sl] = oc
        kaugT[128:192, sl] = oc
        kaugT[192:256, sl] = ((f & 31) == row).astype(f32).astype(bf16)


def fwd_kernel(sc_ref, qT_ref, tab_ref, *rest, R, bk, first, last, nt, n):
    kvs, rest = rest[:n], rest[n:]
    if first:
        rest = (None, None) + rest
    oi_ref, mli_ref, o_ref, ml_ref, *rest = rest
    KB = kvs[0].shape[1]
    bq = qT_ref.shape[1]
    hi, qi = pl.program_id(0), pl.program_id(1)
    if last:
        kaug, vaug, och = rest[-3:]
    else:
        kaug, vaug = rest[-2:]

    for g, kv in enumerate(kvs):

        @pl.when((qi == 0) & (hi == g))
        def _(kv=kv):
            build_kaug(kv[0:64, :], kaug)
            vaug[0:64, :] = kv[64:128, :]
            vaug[64:80, :] = (iota((16, KB), 0) == 0).astype(f32).astype(bf16)

    qaug = make_qaug(qT_ref[...], tab_ref[:, :256], qi * (bq // 64), sc_ref[0], R)
    if first:
        m = jnp.full((1, bq), -3e38, f32)
        o = jnp.zeros((80, bq), f32)
    else:
        m = mli_ref[0:1, :]
        o = jnp.concatenate([oi_ref[...], jnp.broadcast_to(mli_ref[1:2, :], (16, bq))], 0)
    for c in range(KB // bk):
        s = dot(kaug[c * bk : (c + 1) * bk, :], qaug, 1, 1)
        mn = jnp.maximum(m, jnp.max(s, axis=0, keepdims=True))
        al = jnp.exp(m - mn)
        p = jnp.exp(s - mn).astype(bf16)
        o = o * al + jnp.dot(vaug[:, c * bk : (c + 1) * bk], p, preferred_element_type=f32)
        m = mn
    l = o[64:65, :]
    o = o[:64]
    if last:
        o = o * (1.0 / l)
        m = m + jnp.log(l)
        N = och.shape[2]
        ob = o.astype(bf16)
        for j in range(bq // N):
            och[qi * (bq // N) + j] = ob[:, j * N : (j + 1) * N]

        @pl.when(qi == pl.num_programs(1) - 1)
        def _():
            for k in range(nt):
                rest[k][...] = och[sc_ref[1] ^ k]

    o_ref[...] = o
    ml_ref[...] = jnp.concatenate([m, l, jnp.zeros((6, bq), f32)], 0)


def attn_fwd(sc, h0, qT, kvs, tab, state, last, R, nt, bq=2048, bk=512):
    H, _, T = qT.shape
    n = len(kvs)
    KB = kvs[0].shape[1]
    N = T // nt
    bq, bk = min(bq, T), min(bk, KB)
    first = state is None
    qs = lambda r: pl.BlockSpec((None, r, bq), lambda h, i, o: (h0 + h, 0, i))
    ins = [qs(64), pl.BlockSpec((64, 384), lambda h, i, o: (0, 0))]
    ins += [pl.BlockSpec((128, KB), lambda h, i, o: (0, 0))] * n
    ins += [] if first else [qs(64), qs(8)]
    outs = [qs(64), qs(8)]
    shapes = [jax.ShapeDtypeStruct((H, 64, T), f32), jax.ShapeDtypeStruct((H, 8, T), f32)]
    scratch = [pltpu.VMEM((KB, 256), bf16), pltpu.VMEM((80, KB), bf16)]
    if last:
        outs += [pl.BlockSpec((64, N), lambda h, i, o: (h, 0))] * nt
        shapes += [jax.ShapeDtypeStruct((n * 64, N), bf16)] * nt
        scratch += [pltpu.VMEM((nt, 64, N), bf16)]
    return pl.pallas_call(
        functools.partial(fwd_kernel, R=R, bk=bk, first=first, last=last, nt=nt, n=n),
        grid_spec=pltpu.PrefetchScalarGridSpec(
            num_scalar_prefetch=1,
            grid=(n, T // bq),
            in_specs=ins,
            out_specs=outs,
            scratch_shapes=scratch,
        ),
        out_shape=shapes,
        input_output_aliases={} if first else {3 + n: 0, 4 + n: 1},
        compiler_params=pltpu.CompilerParams(vmem_limit_bytes=VMEM),
        cost_estimate=pl.CostEstimate(
            flops=2 * n * T * KB * 512, bytes_accessed=n * T * 1200, transcendentals=n * T * KB
        ),
        name="attn_fwd",
    )(sc, qT, tab, *kvs, *([] if first else state))


def bwd_kernel(sc_ref, qT_ref, tab_ref, *rest, R, bk, has_dq, has_dt, last, nt, n):
    kvs, rest = rest[:n], rest[n:]
    do_refs, rest = rest[:nt], rest[nt:]
    o_ref, ml_ref, *rest = rest
    dqi_ref = dti_ref = dki_ref = None
    if has_dq:
        dqi_ref, *rest = rest
    if has_dt:
        dti_ref, *rest = rest
    if last:
        dki_ref, *rest = rest
        dx_refs, rest = rest[:nt], rest[nt:]
        dt_ref, kaug, kaugT, vaug, acc, dch, fin = rest
    else:
        dq_ref, dkv_ref, dt_ref, kaug, kaugT, vaug, acc, dch = rest
    KB = kvs[0].shape[1]
    bq = qT_ref.shape[1]
    N = dch.shape[2]
    per = bq // N
    hi, qi = pl.program_id(0), pl.program_id(1)

    for g, kv in enumerate(kvs):

        @pl.when((qi == 0) & (hi == g))
        def _(kv=kv):
            build_kaug(kv[0:64, :], kaug, True)
            build_kaugT(kv[0:64, :], kaugT)
            vaug[0:64, :] = kv[64:128, :]
            vaug[64:128, :] = (iota((64, KB), 0) < 3).astype(f32).astype(bf16)

    @pl.when(qi == 0)
    def _():
        if last:
            acc[0:64, :] = dki_ref[0:64, :].astype(f32) * 8.0
            acc[64:128, :] = dki_ref[64:128, :].astype(f32)
        else:
            acc[...] = jnp.zeros_like(acc)
        for k in range(nt):
            dch[sc_ref[1] ^ k] = do_refs[k][...]

    @pl.when((qi == 0) & (hi == 0))
    def _():
        dt_ref[...] = dti_ref[...] if has_dt else jnp.zeros_like(dt_ref)

    qT = qT_ref[...]
    doT = jnp.concatenate([dch[qi * per + j] for j in range(per)], 1)
    il0 = qi * (bq // 64)
    off = sc_ref[0]
    qaug = make_qaug(qT, tab_ref[:, :256], il0, off, R)
    dof = doT.astype(f32)
    nd = -jnp.sum(dof * o_ref[...], axis=0, keepdims=True)
    d1 = nd.astype(bf16).astype(f32)
    d2 = (nd - d1).astype(bf16).astype(f32)
    d3 = nd - d1 - d2
    rid = iota((64, bq), 0)
    ext = jnp.where(rid == 2, d3, jnp.where(rid == 3, ml_ref[0:1, :], 0.0))
    ext = jnp.where(rid == 0, d1, jnp.where(rid == 1, d2, ext))
    t = jnp.concatenate([dof, ext], 0).T
    lse = t[:, 67:68]
    doaug = t.astype(bf16)
    dq = jnp.zeros((bq, 256), f32)
    for c in range(KB // bk):
        sl = slice(c * bk, (c + 1) * bk)
        s = jnp.dot(qaug, kaugT[:, sl], preferred_element_type=f32)
        p = jnp.exp(s - lse)
        dp = jnp.dot(doaug, vaug[:, sl], preferred_element_type=f32)
        pb = p.astype(bf16)
        ds = (p * dp).astype(bf16)
        acc[64:128, sl] += jnp.dot(doT, pb, preferred_element_type=f32)
        acc[0:64, sl] += jnp.dot(qT, ds, preferred_element_type=f32)
        dq += jnp.dot(ds, kaug[sl, :], preferred_element_type=f32)
    lane = iota((64, 128), 1)
    his, los = [], []
    for k in range(bq // 64):
        a = dq[k * 64 : (k + 1) * 64, :128]
        b = dq[k * 64 : (k + 1) * 64, 128:]
        gw = pltpu.roll(jnp.where(lane >= 64, a, 0.0), 64, 1, stride=1, stride_axis=0)
        sh = off - (il0 + k) - 1
        gh = pltpu.roll(
            jnp.where((lane >= 64) & (lane < 64 + R), b, 0.0), lax.rem(sh + 256, 128), 1
        )
        g = jnp.concatenate([gh, gw], 1)
        h = g.astype(bf16)
        his.append(h)
        los.append((g - h.astype(f32)).astype(bf16))
    gh = jnp.concatenate(his, 0)
    gl = jnp.concatenate(los, 0)
    tab = jnp.concatenate([tab_ref[:, :128], tab_ref[:, 256:]], 1)
    dqT = dq[:, :128].T[:64] + dot(tab, gh, 1, 1) + dot(tab, gl, 1, 1)
    if has_dq:
        dqT = dqT + dqi_ref[...]
    dt_ref[...] += dot(qT, gh, 1, 0) + dot(qT, gl, 1, 0)
    if last:
        dqb = dqT.astype(bf16)
        for j in range(per):
            fin[qi * per + j, 0:64, :] = dqb[:, j * N : (j + 1) * N]
    else:
        dq_ref[...] = dqT

    @pl.when(qi == pl.num_programs(1) - 1)
    def _():
        if last:
            for j in range(nt):
                fin[j, 64:128, :] = (acc[0:64, j * N : (j + 1) * N] * 0.125).astype(bf16)
                fin[j, 128:192, :] = acc[64:128, j * N : (j + 1) * N].astype(bf16)
            for k in range(nt):
                dx_refs[k][...] = fin[sc_ref[1] ^ k]
        else:
            dkv_ref[0:64, :] = (acc[0:64, :] * 0.125).astype(bf16)
            dkv_ref[64:128, :] = acc[64:128, :].astype(bf16)


def attn_bwd(sc, h0, qT, kvs, tab, dos, o, ml, dq, dt, back, R, bq=2048, bk=512):
    _, _, T = qT.shape
    n = len(kvs)
    KB = kvs[0].shape[1]
    nt = len(dos)
    N = T // nt
    bq, bk = min(bq, T), min(bk, KB)
    last = back is not None
    qs = lambda r, h0=h0: pl.BlockSpec((None, r, bq), lambda h, i, s: (h0 + h, 0, i))
    fix = lambda shape: pl.BlockSpec(shape, lambda h, i, s: (0, 0))
    ins = [qs(64), fix((64, 384))] + [fix((128, KB))] * n
    ins += [pl.BlockSpec((64, N), lambda h, i, s: (h0 + h, 0))] * nt + [qs(64), qs(8)]
    args = [qT, tab, *kvs, *dos, o, ml]
    if dq is not None:
        ins += [qs(64, dq[1])]
        args += [dq[0]]
    if dt is not None:
        ins += [fix((64, 256))]
        args += [dt]
    scratch = [
        pltpu.VMEM((KB, 256), bf16),
        pltpu.VMEM((256, KB), bf16),
        pltpu.VMEM((128, KB), bf16),
        pltpu.VMEM((128, KB), f32),
        pltpu.VMEM((nt, 64, N), bf16),
    ]
    if last:
        ins += [pl.BlockSpec((None, 128, KB), lambda h, i, s: (back[1], 0, 0))]
        args += [back[0]]
        outs = [fix((192, N))] * nt
        shapes = [jax.ShapeDtypeStruct((192, N), bf16)] * nt
        scratch += [pltpu.VMEM((nt, 192, N), bf16)]
    else:
        outs = [qs(64, 0), pl.BlockSpec((None, 128, KB), lambda h, i, s: (h, 0, 0))]
        shapes = [jax.ShapeDtypeStruct((n, 64, T), f32), jax.ShapeDtypeStruct((n, 128, KB), bf16)]
    return pl.pallas_call(
        functools.partial(
            bwd_kernel, R=R, bk=bk, has_dq=dq is not None, has_dt=dt is not None, last=last,
            nt=nt, n=n,
        ),
        grid_spec=pltpu.PrefetchScalarGridSpec(
            num_scalar_prefetch=1,
            grid=(n, T // bq),
            in_specs=ins,
            out_specs=outs + [fix((64, 256))],
            scratch_shapes=scratch,
        ),
        out_shape=shapes + [jax.ShapeDtypeStruct((64, 256), f32)],
        compiler_params=pltpu.CompilerParams(vmem_limit_bytes=VMEM),
        cost_estimate=pl.CostEstimate(
            flops=(2 if dt is not None else 40) * n * T * KB * 1280, bytes_accessed=n * T * 3000, transcendentals=n * T * KB
        ),
        name="attn_bwd",
    )(sc, *args)


def rows_of(sc_ref, r, dd):
    return pl.ds(pl.multiple_of((sc_ref[2] ^ r) * dd, dd), dd)


def whole_spec(shape):
    return pl.BlockSpec(shape, lambda *_: (0,) * len(shape))


def norm_parts(x):
    c = x - jnp.mean(x, axis=-1, keepdims=True)
    r = lax.rsqrt(jnp.mean(c * c, axis=-1, keepdims=True) + EPS)
    return c * r, r


def norm_back(dh, gain, xhat, r):
    e = dh * gain
    return (
        e - jnp.mean(e, axis=-1, keepdims=True) - xhat * jnp.mean(e * xhat, axis=-1, keepdims=True)
    ) * r


def call(kernel, sc, grid, ins, args, outs, shapes, scratch, name, flops, nbytes):
    return pl.pallas_call(
        kernel,
        grid_spec=pltpu.PrefetchScalarGridSpec(
            num_scalar_prefetch=1, grid=grid, in_specs=ins, out_specs=outs, scratch_shapes=scratch
        ),
        out_shape=[jax.ShapeDtypeStruct(s, d) for s, d in shapes],
        compiler_params=pltpu.CompilerParams(vmem_limit_bytes=VMEM),
        cost_estimate=pl.CostEstimate(flops=flops, bytes_accessed=nbytes, transcendentals=0),
        name=name,
    )(sc, *args)


def pack_kernel(sc_ref, w, rh, rw, n1g, n1b, n2g, n2b, pb, ob, qb, out):
    dd, E3 = w.shape[1], 3 * w.shape[2]
    for h in range(E3 // 192):
        cols = [w[j, :, h * 64 : (h + 1) * 64].astype(f32) for j in range(3)]
        out[0:dd, h * 192 : (h + 1) * 192] = jnp.concatenate(cols, 1).astype(bf16)
    out[dd:, :] = jnp.zeros((32, E3), bf16)
    L = rh.shape[1]
    t, l = iota((L, 128), 0), iota((L, 128), 1)
    back = (t == L - 1 - l).astype(f32).astype(bf16)
    same = (t == l).astype(f32).astype(bf16)
    out[dd : dd + 16, 0:128] = dot(rh[...], back, 1, 0).astype(bf16)
    out[dd : dd + 16, 128:256] = dot(rw[...], back, 1, 0).astype(bf16)
    out[dd : dd + 16, 256:384] = dot(rw[...], same, 1, 0).astype(bf16)
    rows = [v[...].astype(f32).reshape(1, dd) for v in (n1g, n1b, n2g, n2b, pb, ob)]
    rows = jnp.concatenate(rows + [jnp.zeros((10, dd), f32)], 0)
    out[dd + 16 :, 0:dd] = rows.astype(bf16)
    q = [qb[h].astype(f32) for h in range(qb.shape[0])]
    q = jnp.concatenate(q + [jnp.zeros((16 - 2 * len(q), 16), f32)], 0)
    out[dd + 16 :, 256:272] = q.astype(bf16)


def front_kernel(sc_ref, x_ref, s0, s1, s2, s3, tab_ref, v_ref, q_ref, *rest, H):
    kvs, (wt_ref, xh_ref, wn, all4, bias) = rest[:H], rest[H:]
    dd = s0.shape[0] - 32

    @pl.when(pl.program_id(0) == 0)
    def _():
        for r, s in enumerate((s0, s1, s2, s3)):
            all4[sc_ref[2] ^ r] = s[dd:, :]
            wn[rows_of(sc_ref, r, dd), :] = s[0:dd, :]
        wt_ref[...] = wn[...].T
        for j in range(4):
            tab_ref[j * 16 : (j + 1) * 16, :] = all4[j, 0:16, 0:384]
        low = [all4[j, 16:32, :].astype(f32) for j in range(4)]
        v_ref[...] = jnp.concatenate([z[0:8, 0:dd] for z in low], 1)
        q = jnp.concatenate([z[:, 256:272] for z in low] + [jnp.zeros((16, 64), f32)], 1)
        q = q.T[0:64]
        for h in range(H):
            bias[h * 192 : h * 192 + 64, :] = q[:, 2 * h : 2 * h + 1]
            bias[h * 192 + 64 : h * 192 + 128, :] = jnp.zeros((64, 1), f32)
            bias[h * 192 + 128 : (h + 1) * 192, :] = q[:, 2 * h + 1 : 2 * h + 2]

    xh, _ = norm_parts(x_ref[...].astype(f32))
    xh_ref[...] = xh.astype(bf16)
    h1 = (xh * v_ref[0:1, :] + v_ref[1:2, :]).astype(bf16)
    y = dot(wt_ref[...], h1, 1, 1) + bias[...]
    y = y.astype(bf16)
    for h in range(H):
        q_ref[h] = y[h * 192 : h * 192 + 64]
        kvs[h][...] = y[h * 192 + 64 : (h + 1) * 192]


def front(sc, x, ss, H):
    T, D = x.shape
    E3 = H * 192
    bt = min(512, T)
    rows = pl.BlockSpec((bt, D), lambda i, s: (i, 0))
    return call(
        functools.partial(front_kernel, H=H), sc, (T // bt,),
        [rows] + [whole_spec(ss[0].shape)] * 4, [x, *ss],
        [whole_spec((64, 384)), whole_spec((8, D))]
        + [pl.BlockSpec((H, 64, bt), lambda i, s: (0, 0, i))]
        + [pl.BlockSpec((128, bt), lambda i, s: (0, i))] * H
        + [whole_spec((E3, D)), rows],
        [((64, 384), bf16), ((8, D), f32), ((H, 64, T), bf16)]
        + [((128, T), bf16)] * H
        + [((E3, D), bf16), ((T, D), bf16)],
        [pltpu.VMEM((D, E3), bf16), pltpu.VMEM((4, 32, E3), bf16), pltpu.VMEM((E3, 1), f32)],
        "front", 2 * T * D * E3, 6 * T * D,
    )


def mlpa_kernel(sc_ref, x_ref, v_ref, *rest, nt, fb):
    no = 2 * nt
    os, ps, p1, rest = rest[:no], rest[no : no + 4], rest[no + 4], rest[no + 5 :]
    a_ref, sl_ref, h2_ref, y1_ref, wt_ref, wp, b4, bias = rest
    dd, ft = p1.shape[1:]
    D = 4 * dd
    k = pl.program_id(0)

    @pl.when(k == 0)
    def _():
        y = x_ref[...].astype(f32) + v_ref[4:5, :]
        na = os[0].shape[0]
        for kk in range(nt):
            for r in range(4):
                wp[rows_of(sc_ref, r, dd), :] = ps[r][kk, 0:dd]
            wt = wp[...].T
            wt_ref[kk] = wt
            y = y + dot(os[kk][...], wt[:na], 0, 0)
            y = y + dot(os[nt + kk][...], wt[na:], 0, 0)
        y1_ref[...] = y
        xh, _ = norm_parts(y)
        h2_ref[...] = (xh * v_ref[2:3, :] + v_ref[3:4, :]).astype(bf16)

    for r in range(4):
        b4[sc_ref[2] ^ r] = ps[r][k, dd:, :].astype(f32)
    rows = jnp.concatenate([b4[j, :, 0:16] for j in range(4)], 1)
    for i in range(ft // 64):
        bias[:, i * 64 : (i + 1) * 64] = rows[i : i + 1]
    for j in range(ft // fb):
        sl = slice(j * fb, (j + 1) * fb)
        wi = p1[:, :, sl].reshape(D, fb)
        u = jnp.dot(h2_ref[...], wi, preferred_element_type=f32) + bias[:, sl]
        cdf = 0.5 + 0.5 * lax.erf(u * 0.7071067811865476)
        a_ref[:, sl] = (u * cdf).astype(bf16)
        slope = cdf + u * (jnp.exp(-0.5 * u * u) * 0.3989422804014327)
        sl_ref[:, sl] = slope.astype(sl_ref.dtype)


def back_block(nd, rows, cols):
    return pl.BlockSpec((nd, None, rows, cols), lambda k, s: (0, s[1] ^ k, 0, 0))


def mlpa(sc, x, vecs, os, ps, p1):
    D = x.shape[1]
    nd, nt, dd, ft = p1.shape
    N = os[0].shape[1]
    kt = ps[0].shape[2]
    mine = pl.BlockSpec((N, D), lambda k, s: (s[1], 0))
    act = pl.BlockSpec((None, N, ft), lambda k, s: (k, 0, 0))
    full = whole_spec((N, D))
    return call(
        functools.partial(mlpa_kernel, nt=nt, fb=256), sc, (nt,),
        [mine, whole_spec(vecs.shape)]
        + [whole_spec(o.shape) for o in os]
        + [whole_spec(p.shape) for p in ps]
        + [back_block(nd, dd, ft)],
        [x, vecs, *os, *ps, p1],
        [act, act, full, full, whole_spec((nt, kt, D))],
        [((nt, N, ft), bf16), ((nt, N, ft), f32), ((N, D), bf16), ((N, D), f32)]
        + [((nt, kt, D), bf16)],
        [pltpu.VMEM((D, kt), bf16), pltpu.VMEM((4, 16, kt), f32), pltpu.VMEM((1, ft), f32)],
        "mlp_in", 3 * N * D * ft * nt, 24 * 2**20,
    )


def mlpb_kernel(sc_ref, g_ref, v_ref, y1_ref, sl_ref, *rest, nt, fb):
    wt_ref, p1, p2, du_ref, da_ref, dy_ref, sm_ref, db_ref, *dos, dh = rest
    D, ft = p1.shape[0] * p1.shape[1], p1.shape[2]
    k = pl.program_id(0)

    @pl.when(k == 0)
    def _():
        dh[...] = jnp.zeros_like(dh)

    for j in range(ft // fb):
        sl = slice(j * fb, (j + 1) * fb)
        ga = jnp.dot(g_ref[...], p2[:, :, sl].reshape(D, fb), preferred_element_type=f32)
        du = (sl_ref[:, sl] * ga).astype(bf16)
        du_ref[:, sl] = du
        db_ref[:, sl] = jnp.sum(du.astype(f32), axis=0, keepdims=True)
        dh[...] += dot(du, p1[:, :, sl].reshape(D, fb), 1, 1)

    @pl.when(k == pl.num_programs(0) - 1)
    def _():
        g = g_ref[...].astype(f32)
        xh, r = norm_parts(y1_ref[...])
        d = dh[...]
        dy = g + norm_back(d, v_ref[2:3, :], xh, r)
        dy_ref[...] = dy
        da = dy.astype(bf16)
        da_ref[...] = da
        sums = [jnp.sum(z, axis=0, keepdims=True) for z in (d * xh, d, da.astype(f32), g)]
        sm_ref[...] = jnp.concatenate(sums + [jnp.zeros((4, D), f32)], 0)
        for kk in range(nt):
            dos[kk][...] = dot(wt_ref[kk], da, 1, 1).astype(bf16)


def mlpb(sc, g, vecs, y1, slope, wt, p1, p2):
    N, D = y1.shape
    nd, nt, dd, ft = p1.shape
    kt = wt.shape[1]
    act = pl.BlockSpec((None, N, ft), lambda k, s: (k, 0, 0))
    row = pl.BlockSpec((None, 1, ft), lambda k, s: (s[1] ^ k, 0, 0))
    full = whole_spec((N, D))
    return call(
        functools.partial(mlpb_kernel, nt=nt, fb=256), sc, (nt,),
        [pl.BlockSpec((N, D), lambda k, s: (s[1], 0)), whole_spec(vecs.shape), full, act]
        + [whole_spec(wt.shape)]
        + [back_block(nd, dd, ft)] * 2,
        [g, vecs, y1, slope, wt, p1, p2],
        [act, full, full, whole_spec((8, D)), row] + [whole_spec((kt, N))] * nt,
        [((nt, N, ft), bf16), ((N, D), bf16), ((N, D), f32), ((8, D), f32), ((nt, 1, ft), f32)]
        + [((kt, N), bf16)] * nt,
        [pltpu.VMEM((N, D), f32)],
        "mlp_grad", 5 * N * D * ft * nt, 24 * 2**20,
    )


def mlp2_kernel(sc_ref, g_ref, v_ref, h2_ref, da_ref, y_ref, a_ref, du_ref, *rest, nt):
    no = 2 * nt
    os, (p2, *rest) = rest[:no], rest[no:]
    gws, (out_ref, hT, gT, dT, oa, acc, acn) = rest[:4], rest[4:]
    ft = a_ref.shape[1]
    D = h2_ref.shape[1]
    dd = D // 4
    k = pl.program_id(0)

    @pl.when(k == 0)
    def _():
        for src, dst in ((h2_ref, hT), (g_ref, gT), (da_ref, dT)):
            acn[...] = src[...].astype(f32).T
            for r in range(4):
                dst[r * dd : (r + 1) * dd, :] = acn[rows_of(sc_ref, r, dd), :].astype(bf16)
        na = os[0].shape[0]
        for kk in range(nt):
            oa[kk, :na] = os[kk][...]
            oa[kk, na:] = os[nt + kk][...]
        acc[...] = jnp.zeros_like(acc)

    a = a_ref[...]
    acc[...] += dot(a, p2[...].reshape(D, ft), 1, 1)

    def store(value, lo, hi):
        value = value.astype(bf16)
        for r in range(4):
            gws[r][:, lo:hi] = value[r * dd : (r + 1) * dd]

    store(jnp.dot(hT[...], du_ref[...], preferred_element_type=f32), 0, ft)
    store(jnp.dot(gT[...], a, preferred_element_type=f32), ft, 2 * ft)
    store(dot(dT[...], oa[k], 1, 1), 2 * ft, gws[0].shape[1])

    @pl.when(k == pl.num_programs(0) - 1)
    def _():
        out_ref[...] = (y_ref[...] + (acc[...] + v_ref[5:6, :])).astype(bf16)


def mlp2(sc, g, vecs, h2, da, y1, a, du, os, p2):
    N, D = h2.shape
    nd, nt, dd, ft = p2.shape
    kt = os[0].shape[0] + os[nt].shape[0]
    cols = 2 * ft + kt
    full = whole_spec((N, D))
    act = pl.BlockSpec((None, N, ft), lambda k, s: (k, 0, 0))
    gw = pl.BlockSpec((None, dd, cols), lambda k, s: (s[1] ^ k, 0, 0))
    return call(
        functools.partial(mlp2_kernel, nt=nt), sc, (nt,),
        [pl.BlockSpec((N, D), lambda k, s: (s[1], 0)), whole_spec(vecs.shape), full, full, full]
        + [act, act]
        + [whole_spec(o.shape) for o in os]
        + [back_block(nd, dd, ft)],
        [g, vecs, h2, da, y1, a, du, *os, p2],
        [gw] * 4 + [full],
        [((nt, dd, cols), bf16)] * 4 + [((N, D), bf16)],
        [pltpu.VMEM((D, N), bf16)] * 3
        + [pltpu.VMEM((nt, kt, N), bf16), pltpu.VMEM((N, D), f32), pltpu.VMEM((D, N), f32)],
        "mlp_weights", 7 * N * D * ft * nt, 24 * 2**20,
    )


def gqkv_kernel(sc_ref, x_ref, v_ref, wt_ref, *rest, nt, H):
    dx, (keep_ref, send_ref, b_ref, n_ref, g) = rest[: H * nt], rest[H * nt :]
    dd = keep_ref.shape[1]
    lane = iota((192, 128), 1)
    gain, shift = v_ref[0:1, :], v_ref[1:2, :]
    dg, db = jnp.zeros_like(gain), jnp.zeros_like(gain)
    for h in range(H):
        t = jnp.zeros((192, x_ref.shape[2]), f32)
        b = jnp.zeros((192, 1), f32)
        for k in range(nt):
            d = dx[h * nt + k][...]
            t = t + jnp.dot(d, x_ref[sc_ref[1] ^ k], preferred_element_type=f32)
            b = b + jnp.sum(d.astype(f32), axis=1, keepdims=True)
        w = wt_ref[h * 192 : (h + 1) * 192, :].astype(f32)
        dg = dg + jnp.sum(w * t, axis=0, keepdims=True)
        db = db + jnp.sum(w * b, axis=0, keepdims=True)
        g[:, h * 192 : (h + 1) * 192] = (t * gain + shift * b).T.astype(bf16)
        b_ref[h] = jnp.where(lane == 0, b, 0.0)
    n_ref[...] = jnp.concatenate([dg, db, jnp.zeros((6, dg.shape[1]), f32)], 0)
    for r in range(4):
        dst = send_ref if r & 1 else keep_ref
        dst[r // 2] = g[rows_of(sc_ref, r, dd), :]


def gqkv(sc, xh, vecs, wT, dx, nt):
    T, D = xh.shape
    H = len(dx) // nt
    N = T // nt
    dd = D // 4
    part = (2, dd, H * 192)
    return call(
        functools.partial(gqkv_kernel, nt=nt, H=H), sc, (1,),
        [whole_spec((nt, N, D)), whole_spec(vecs.shape), whole_spec(wT.shape)]
        + [whole_spec((192, N))] * len(dx),
        [xh.reshape(nt, N, D), vecs, wT, *dx],
        [whole_spec(part), whole_spec(part), whole_spec((H, 192, 128)), whole_spec((8, D))],
        [(part, bf16), (part, bf16), ((H, 192, 128), f32), ((8, D), f32)],
        [pltpu.VMEM((D, H * 192), bf16)],
        "qkv_weights", 2 * T * D * 192 * H, 8 * 2**20,
    )


def dh1_kernel(sc_ref, x_ref, dy_ref, v_ref, *rest, nt, H):
    dx, (p3, gi_ref, da) = rest[: H * nt], rest[H * nt :]
    D = x_ref.shape[1]
    E3 = H * 192
    for k in range(nt):
        for h in range(H):
            da[(k * H + h) * 192 : (k * H + h + 1) * 192, :] = dx[h * nt + k][...]
    t = jnp.zeros((D, da.shape[1]), f32)
    for k in range(nt):
        w = p3[:, sc_ref[1] ^ k].reshape(D, E3)
        t = t + jnp.dot(w, da[k * E3 : (k + 1) * E3, :], preferred_element_type=f32)
    xh, r = norm_parts(x_ref[...].astype(f32))
    gi_ref[...] = (dy_ref[...] + norm_back(t.T, v_ref[0:1, :], xh, r)).astype(bf16)


def dh1(sc, x, dy1, vecs, dx, p3):
    N, D = dy1.shape
    nt = p3.shape[1]
    H = len(dx) // nt
    return call(
        functools.partial(dh1_kernel, nt=nt, H=H), sc, (1,),
        [pl.BlockSpec((N, D), lambda k, s: (s[1], 0)), whole_spec((N, D)), whole_spec(vecs.shape)]
        + [whole_spec((192, N))] * len(dx)
        + [whole_spec(p3.shape)],
        [x, dy1, vecs, *dx, p3],
        [whole_spec((N, D))],
        [((N, D), bf16)],
        [pltpu.VMEM((nt * H * 192, N), bf16)],
        "norm1_grad", 2 * N * D * D * 3, 8 * 2**20,
    )[0]


def copy_kernel(sc_ref, a, b):
    b[...] = a[...].astype(b.dtype)


def copied(sc, v, dtype):
    rows = pl.BlockSpec((v.shape[0] // 4, v.shape[1]), lambda i, s: (i, 0))
    return call(
        copy_kernel, sc, (4,), [rows], [v], [rows], [(v.shape, dtype)], [], "copied", 0, 2**22
    )[0]


def shift(value, axis, steps):
    n = lax.axis_size(axis)
    return lax.ppermute(value, axis, [(s, (s + steps) % n) for s in range(n)])


def flip(value, axis, bit):
    n = lax.axis_size(axis)
    return lax.ppermute(value, axis, [(s, s ^ bit) for s in range(n)])


def after(value, *others):
    return lax.optimization_barrier((value, *others))[0]


def gather_weights(shard):
    nd, nt = lax.axis_size("dp"), lax.axis_size("tensor")
    return lax.all_gather(shard, ("dp", "tensor")).reshape((nd, nt) + shard.shape)


def spread(parts):
    return [parts[0]] + [flip(p, "tensor", k) for k, p in enumerate(parts) if k]


def total_ctx(value):
    v = value.astype(bf16)
    if lax.axis_size("ctx") == 2:
        return v.astype(f32) + flip(v, "ctx", 1).astype(f32)
    return lax.psum(v.astype(f32), "ctx")


def per_device(
    block_input,
    cotangent,
    norm1_gain,
    norm1_bias,
    qkv_weight,
    qkv_bias,
    rel_pos_h,
    rel_pos_w,
    proj_weight,
    proj_bias,
    norm2_gain,
    norm2_bias,
    mlp_in_weight,
    mlp_in_bias,
    mlp_out_weight,
    mlp_out_bias,
):
    nt, nc = lax.axis_size("tensor"), lax.axis_size("ctx")
    me, pos, dp = lax.axis_index("tensor"), lax.axis_index("ctx"), lax.axis_index("dp")
    T, D = block_input.shape[1:]
    R = T // GW
    dd = D // 4
    N = T // nt
    H = qkv_bias.shape[1]
    E = H * HD
    L = rel_pos_h.shape[0]
    ft = mlp_in_weight.shape[1]
    x2 = block_input.reshape(T, D)
    g2 = cotangent.reshape(T, D)

    def scalars(k):
        off = (((pos - k) % nc) - pos) * R
        return jnp.stack([off, me, dp]).astype(jnp.int32)

    sc = scalars(0)
    bar = lax.optimization_barrier

    smalls = [qkv_weight.transpose(1, 0, 2), rel_pos_h.T, rel_pos_w.T]
    smalls += [norm1_gain, norm1_bias, norm2_gain, norm2_bias, proj_bias, mlp_out_bias]
    smalls += [qkv_bias.transpose(1, 0, 2)]
    small = call(
        pack_kernel, sc, (1,), [whole_spec(v.shape) for v in smalls], smalls,
        [whole_spec((dd + 32, 3 * E))], [((dd + 32, 3 * E), bf16)], [], "pack", 0, 2**16,
    )[0]
    p1 = gather_weights(mlp_in_weight)
    p2 = gather_weights(mlp_out_weight.T)
    brow = jnp.pad(mlp_in_bias, ((0, 16 - mlp_in_bias.shape[0]), (0, E - 16)))
    own = jnp.concatenate([proj_weight.T, brow], 0)
    near = flip(own, "tensor", 1)
    small = [small] + [flip(small, "dp", r) for r in (1, 2, 3)]
    near, small = bar((near, small))
    own = jnp.stack([own, near])
    two = flip(own, "tensor", 2)

    tab, vecs, qT, *rest = front(sc, x2, small, H)
    kvs, (wT, xh1) = rest[:H], rest[H:]
    kv_far = [[shift(kv, "ctx", k) for kv in kvs] for k in range(1, nc)]

    state = attn_fwd(sc, 0, qT, kvs, tab, None, False, R, nt)
    state, two = bar((state, two))
    own = jnp.concatenate([own, two])
    far = flip(own, "dp", 2)
    for k in range(1, nc - 1):
        state = attn_fwd(scalars(k), 0, qT, kv_far[k - 1], tab, state, False, R, nt)
    os = []
    for h0, h1 in ((0, H - 1), (H - 1, H)):
        *state, o0, o1, o2, o3 = attn_fwd(
            scalars(nc - 1), h0, qT, kv_far[-1][h0:h1], tab, state, True, R, nt
        )
        if h0 == 0:
            state, far = bar((state, far))
            ps = [own, flip(own, "dp", 1), far, flip(far, "dp", 1)]
        else:
            o0, ps = bar((o0, ps))
        os += spread([o0, o1, o2, o3])
    o32, lse = state
    p3 = gather_weights(after(small[0], *os)[:dd])
    a, slope, h2, y1, wt = mlpa(sc, x2, vecs, os, ps, p1)
    du, da, dy1, sm2, dbin, *dos = mlpb(sc, g2, vecs, y1, slope, wt, p1, p2)
    dos = spread(dos)
    *gws, out = mlp2(sc, g2, vecs, h2, da, y1, a, du, os, p2)

    add = lambda *v: sum(z.astype(f32) for z in v).astype(bf16)
    out, dos, p3 = bar((out, dos, p3))
    core = [flip(gws[1], "dp", 1), flip(gws[3], "dp", 1)]
    halves = nc == 2
    part = lambda v, i: lax.dynamic_index_in_dim(
        v.reshape(v.shape[:-2] + (2, dd // 2, v.shape[-1])), i, v.ndim - 2, keepdims=False
    )
    dtab = None
    dqs, backs = [], []
    for h0, h1 in ((0, 1), (1, H)):
        back, dq = None, None
        for k in range(1, nc):
            dq, dkv, dtab = attn_bwd(
                scalars(k), h0, qT, kv_far[k - 1][h0:h1], tab, dos, o32, lse, dq, dtab, None, R
            )
            dq = (dq, 0)
            dkv = shift(dkv, "ctx", -k)
            back = dkv if back is None else add(back, dkv)
        dqs += [(dq[0], i) for i in range(h1 - h0)]
        backs += [(back, i) for i in range(h1 - h0)]
        if h0 == 0:
            dtab, core = bar((dtab, core))
            pair = [add(gws[0], core[0]), add(gws[2], core[1])]
            if halves:
                xa = flip(pair[1][: nt // 2], "dp", 2)
                low = jnp.concatenate([z[nt // 2 :] for z in pair])
                yb = flip(part(low, 1 - pos), "ctx", 1)
            else:
                xa = flip(pair[1], "dp", 2)
    block_out = lax.all_gather(out.reshape(1, N, D), "tensor", axis=1, tiled=True)
    if halves:
        dtab, xa, yb = bar((dtab, xa, yb))
        va = add(pair[0][: nt // 2], xa)
        vb = add(part(low, pos), yb)
        ya = flip(part(va, 1 - pos), "ctx", 1)
        xb = flip(vb[nt // 2 :], "dp", 2)
    else:
        dtab, xa = bar((dtab, xa))
        v = add(pair[0], xa)
    dx, dxr = [], []
    for h in range(H):
        *d, dtab = attn_bwd(
            sc, h, qT, kvs[h : h + 1], tab, dos, o32, lse, dqs[h], dtab, backs[h], R
        )
        dx += d
        if h == 0 and halves:
            dtab, xb = bar((dtab, xb))
        if h == 1:
            if halves:
                dtab, ya = bar((dtab, ya))
                v = jnp.concatenate([add(part(va, pos), ya), add(vb[: nt // 2], xb)])
            dtab, dxr, v = bar((dtab, dxr, v))
        if h == 2:
            dtab, dxr, xh1 = bar((dtab, dxr, xh1))
        dxr = dxr + spread(d)
    gsum = lax.psum_scatter(v, "tensor", scatter_dimension=0)

    keepq, sendq, bq, sm1 = gqkv(sc, xh1, vecs, wT, dx, nt)

    tid = jnp.arange(nt)
    bq = bq[:, :, 0].reshape(H, 3, HD)
    bq = jnp.stack([bq[:, 0], bq[:, 2]]).reshape(1, 2 * E)
    bq = jnp.where(tid[:, None] == me, bq, 0.0)
    flat = jnp.concatenate(
        [z.reshape(-1, 256) for z in (sm2[:4], sm1[:2], dbin, bq)] + [dtab]
    )
    flat, sendq, dxr = bar((flat, sendq, dxr))
    flats = [flat] + [flip(flat, "tensor", k) for k in range(1, nt)]

    gin = dh1(sc, x2, dy1, vecs, dxr, p3)
    gin, sendq, flats = bar((gin, sendq, flats))
    gall = lax.all_gather(gin, "tensor", axis=0, tiled=True)
    while len(flats) > 1:
        flats = [flats[i] + flats[i + 1] for i in range(0, len(flats), 2)]
    flat = flats[0] + flip(flats[0], "dp", 1)
    flat = flat + flip(flat, "dp", 2)
    flat = flat + flip(flat, "ctx", 1) if nc == 2 else lax.psum(flat, "ctx")

    coreq = flip(sendq, "dp", 1)
    if halves:
        gsum = gsum.astype(bf16)
        other = flip(gsum, "ctx", 1)
        gmine = jnp.concatenate(
            [jnp.where(pos == 0, gsum, other), jnp.where(pos == 0, other, gsum)], 0
        ).astype(f32)
    else:
        gmine = total_ctx(gsum)
    g_in = gmine[:, :ft]
    g_out = gmine[:, ft : 2 * ft].T
    g_proj = gmine[:, 2 * ft :].T
    farq = flip(add(keepq[1], coreq[1]), "dp", 2)
    gq = total_ctx(add(keepq[0], coreq[0], farq))
    g_qkv = gq.reshape(dd, H, 3, HD).transpose(0, 2, 1, 3).reshape(dd, 3, E)

    vec = flat[: 6 * D // 256].reshape(6, 4, dd)
    vec = lax.dynamic_index_in_dim(vec, dp, 1, keepdims=False)
    at = 6 * D // 256
    gb = flat[at : at + nt * ft // 256].reshape(nt, ft // 64, 4, 16)
    gb = lax.dynamic_index_in_dim(gb, me, 0, keepdims=False)
    gb = lax.dynamic_index_in_dim(gb, dp, 1, keepdims=False)
    at += nt * ft // 256
    gbq = flat[at : at + nt * 2 * E // 256].reshape(nt, 2, H, 4, 16)
    gbq = lax.dynamic_index_in_dim(gbq, me, 0, keepdims=False)
    gbq = lax.dynamic_index_in_dim(gbq, dp, 2, keepdims=False)
    at += nt * 2 * E // 256
    gtab = lax.dynamic_index_in_dim(flat[at:].reshape(4, 16, 2, 128), dp, 0, keepdims=False)
    gtab_h, gtab_w = gtab[:, 0, :L][:, ::-1].T, gtab[:, 1, :L].T
    block_out = copied(sc, after(block_out, gin).reshape(T, D), bf16)
    gall, vec, block_out, g_qkv, gbq, gtab_h, gtab_w, gb, g_in, g_out, g_proj = bar(
        (gall, vec, block_out, g_qkv, gbq, gtab_h, gtab_w, gb, g_in, g_out, g_proj)
    )
    grad_input = gall.astype(f32).reshape(1, T, D)
    return (
        block_out.reshape(1, T, D),
        grad_input,
        vec[4],
        vec[5],
        g_qkv,
        gbq,
        gtab_h,
        gtab_w,
        g_proj,
        vec[2],
        vec[0],
        vec[1],
        g_in,
        gb,
        g_out,
        vec[3],
    )


def solution(mesh):
    placed = (
        P("dp", "ctx", None),
        P("dp", "ctx", None),
        P("dp"),
        P("dp"),
        P("dp", None, "tensor"),
        P(None, "tensor", "dp"),
        P(None, "dp"),
        P(None, "dp"),
        P("tensor", "dp"),
        P("dp"),
        P("dp"),
        P("dp"),
        P("dp", "tensor"),
        P("tensor", "dp"),
        P("tensor", "dp"),
        P("dp"),
    )
    return jax.shard_map(
        per_device,
        mesh=mesh,
        in_specs=placed,
        out_specs=(placed[0], placed[0]) + placed[2:],
        check_vma=False,
    )
```

profile of v0, /device:TPU:0, one launch (start us, length us, event | category | flops | bytes accessed | tf_op | source)
XLA Modules:
  0.0 454.6 jit_solution(7117837741064682862)
XLA Ops:
  22.8 8.9 %collective-permute-done.3.s3 = bf16[224,576]{1,0:T(8,128)(2,1)S(1)} collective-permute-done((bf16[224,576]{1,0:T(8,128)(2,1)}, bf16[224,576]{1,0:T(8,128)(2,1)S(1)}, u32[]{:S(2)}, u32[]{:S(2)}) %collective-permute-start.3) | collective-permute-done | bytes 258080 | tf_op jit(solution)/shard_map/ppermute | solution.py:716
  34.4 8.8 %front.1 = (bf16[64,384]{1,0:T(8,128)(2,1)}, f32[8,768]{1,0:T(8,128)}, bf16[3,64,2048]{2,1,0:T(8,128)(2,1)}, bf16[128,2048]{1,0:T(8,128)(2,1)}, bf16[128,2048]{1...) custom-call(s32[3]{0:T(128)} %add_add_fusion.1.sc_ref, ...), custom_call_target="tpu_custom_call" | custom-call | flops 1811939328 | bytes 9437184 | tf_op jit(solution)/shard_map/front/pallas_call | solution.py:361
  46.8 23.6 %attn_fwd.3 = (f32[3,64,2048]{2,1,0:T(8,128)}, f32[3,8,2048]{2,1,0:T(8,128)}) custom-call(s32[3]{0:T(128)} %add_add_fusion.1.sc_ref, bf16[3,64,2048]{2,1,0:T(8,128)(2,1)} %get-tuple-element.168.qT_ref, bf16[64,384]{1,0:T(8,128)(2,1)} %get-tuple-element.169.tab_ref, bf16[128,2048]{1,0:T(8,128)(2,1)} %get-tuple-element.170.rest_0_, ...), custom_call_target="tpu_custom_call" | custom-call | flops 12884901888 | bytes 7372800 | tf_op jit(solution)/shard_map/attn_fwd/pallas_call | solution.py:152
  73.9 19.8 %attn_fwd.4 = (f32[3,64,2048]{2,1,0:T(8,128)}, f32[3,8,2048]{2,1,0:T(8,128)}, bf16[128,512]{1,0:T(8,128)(2,1)}, bf16[128,512]{1,0:T(8,128)(2,1)}, bf16[128,512]{1,0:T(8,128)(2,1)}, /*index=5*/bf16[128,512]{1,0:T(8,128)(2,1)}) custom-call(s32[3]{0:T(128)} %add_add_fusion.2.sc_ref, ...), custom_call_target="tpu_custom_call", output_to_operand_aliasing={{0}: (5, {}), {1}: (6, {})} | custom-call | flops 8589934592 | bytes 4915200 | tf_op jit(solution)/shard_map/attn_fwd/pallas_call | solution.py:152
  95.2 10.2 %attn_fwd.5 = (f32[3,64,2048]{2,1,0:T(8,128)}, f32[3,8,2048]{2,1,0:T(8,128)}, bf16[64,512]{1,0:T(8,128)(2,1)}, bf16[64,512]{1,0:T(8,128)(2,1)}, bf16[64,512]{1,0:T(8,128)(2,1)}, /*index=5*/bf16[64,512]{1,0:T(8,128)(2,1)}) custom-call(s32[3]{0:T(128)} %add_add_fusion.2.sc_ref, ...), custom_call_target="tpu_custom_call", output_to_operand_aliasing={{0}: (4, {}), {1}: (5, {})} | custom-call | flops 4294967296 | bytes 2457600 | tf_op jit(solution)/shard_map/attn_fwd/pallas_call | solution.py:152
  107.5 3.9 collective-permute-start.9
  111.4 5.9 %collective-permute-done.14.rest_5_ = bf16[64,512]{1,0:T(8,128)(2,1)S(1)} collective-permute-done((bf16[64,512]{1,0:T(8,128)(2,1)}, bf16[64,512]{1,0:T(8,128)(2,1)S(1)}, u32[]{:S(2)}, u32[]{:S(2)}) %collective-permute-start.14) | collective-permute-done | bytes 65568 | tf_op jit(solution)/shard_map/ppermute | solution.py:716
  119.5 20.5 %collective-permute-done.15.rest_6_ = bf16[64,512]{1,0:T(8,128)(2,1)S(1)} collective-permute-done((bf16[64,512]{1,0:T(8,128)(2,1)}, bf16[64,512]{1,0:T(8,128)(2,1)S(1)}, u32[]{:S(2)}, u32[]{:S(2)}) %collective-permute-start.15) | collective-permute-done | bytes 65568 | tf_op jit(solution)/shard_map/ppermute | solution.py:716
  141.1 13.3 %mlp_in.1 = (bf16[4,512,768]{2,1,0:T(8,128)(2,1)}, f32[4,512,768]{2,1,0:T(8,128)}, bf16[512,768]{1,0:T(8,128)(2,1)}, f32[512,768]{1,0:T(8,128)}, bf16[4,192,768]{2,1,0:T(8,128)(2,1)}) custom-call(s32[3]{0:T(128)} %add_add_fusion.1.sc_ref, bf16[2048,768]{1,0:T(8,128)(2,1)} %bitcast.94, f32[8,768]{1,0:T(8,128)} %get-tuple-element.167.v_ref, ...), custom_call_target="tpu_custom_call" | custom-call | flops 3623878656 | bytes 25165824 | tf_op jit(solution)/shard_map/mlp_in/pallas_call | solution.py:361
  154.4 16.3 %mlp_grad.1 = (bf16[4,512,768]{2,1,0:T(8,128)(2,1)}, bf16[512,768]{1,0:T(8,128)(2,1)}, f32[512,768]{1,0:T(8,128)}, f32[8,768]{1,0:T(8,128)}, f32[4,1,768]{2,1,0:...) custom-call(s32[3]{0:T(128)} %add_add_fusion.1.sc_ref, ...), custom_call_target="tpu_custom_call" | custom-call | flops 6039797760 | bytes 25165824 | tf_op jit(solution)/shard_map/mlp_grad/pallas_call | solution.py:361
  175.2 16.9 %mlp_weights.1 = (bf16[4,192,1728]{2,1,0:T(8,128)(2,1)}, bf16[4,192,1728]{2,1,0:T(8,128)(2,1)}, bf16[4,192,1728]{2,1,0:T(8,128)(2,1)}, bf16[4,192,1728]{2,1,0:T(8,128)(2,1)}, bf16[512,768]{1,0:T(8,128)(2,1)}) custom-call(s32[3]{0:T(128)} %add_add_fusion.1.sc_ref, bf16[2048,768]{1,0:T(8,128)(2,1)} %bitcast.123, f32[8,768]{1,0:T(8,128)} %get-tuple-element.167.v_ref, ...), custom_call_target="tpu_custom_call" | custom-call | flops 8455716864 | bytes 25165824 | tf_op jit(solution)/shard_map/mlp_weights/pallas_call | solution.py:361
  192.6 14.0 %all-gather.16.cloned.1.call-done = bf16[3072,576]{1,0:T(8,128)(2,1)} async-done(((bf16[192,576]{1,0:T(8,128)(2,1)}), bf16[3072,576]{1,0:T(8,128)(2,1)}) %all-gather.16.cloned.1.call-update) | async-done | bytes 3538960 | tf_op jit(solution)/shard_map/all_gather | solution.py:725
  207.4 14.8 %attn_bwd.5 = (f32[1,64,2048]{2,1,0:T(8,128)}, bf16[1,128,2048]{2,1,0:T(8,128)(2,1)}, f32[64,256]{1,0:T(8,128)}) custom-call(s32[3]{0:T(128)} %add_add_fusion.2.sc_ref, bf16[3,64,2048]{2,1,0:T(8,128)(2,1)} %get-tuple-element.168.qT_ref, bf16[64,384]{1,0:T(8,128)(2,1)} %get-tuple-element.169.tab_ref, bf16[128,2048]{1,0:T(8,128)(2,1)} %copy-done.19, ...), custom_call_target="tpu_custom_call" | custom-call | flops 214748364800 | bytes 6144000 | tf_op jit(solution)/shard_map/attn_bwd/pallas_call | solution.py:318
  223.8 4.7 %add_convert_fusion = (bf16[4,192,1728]{2,1,0:T(8,128)(2,1)S(1)}, bf16[4,192,1728]{2,1,0:T(8,128)(2,1)S(1)}) fusion(bf16[4,192,1728]{2,1,0:T(8,128)(2,1)} %collective-permute-done.20, bf16[4,192,1728]{2,1,0:T(8,128)(2,1)S(1)} %copy-done, bf16[4,192,1728]{2,1,0:T(8,128)(2,1)} %collective-permute-done.21, bf16[4,192,1728]{2,1,0:T(8,128)(2,1)} %get-tuple-element.225), kind=kLoop, calls=%fused_computation | loop fusion | flops 10616832 | bytes 15925248 | tf_op jit(solution)/shard_map/convert_element_type | solution.py:822
  232.2 29.1 %attn_bwd.6 = (f32[2,64,2048]{2,1,0:T(8,128)}, bf16[2,128,2048]{2,1,0:T(8,128)(2,1)}, f32[64,256]{1,0:T(8,128)}) custom-call(s32[3]{0:T(128)} %add_add_fusion.2.sc_ref, bf16[3,64,2048]{2,1,0:T(8,128)(2,1)} %get-tuple-element.168.qT_ref, bf16[64,384]{1,0:T(8,128)(2,1)} %get-tuple-element.169.tab_ref, bf16[128,2048]{1,0:T(8,128)(2,1)} %copy-done.17, ...), custom_call_target="tpu_custom_call" | custom-call | flops 21474836480 | bytes 12288000 | tf_op jit(solution)/shard_map/attn_bwd/pallas_call | solution.py:318
  263.0 3.8 collective-permute-done.23
  271.8 15.1 %attn_bwd.7 = (bf16[192,512]{1,0:T(8,128)(2,1)}, bf16[192,512]{1,0:T(8,128)(2,1)}, bf16[192,512]{1,0:T(8,128)(2,1)}, bf16[192,512]{1,0:T(8,128)(2,1)}, f32[64,256]{1,0:T(8,128)}) custom-call(s32[3]{0:T(128)} %add_add_fusion.1.sc_ref, bf16[3,64,2048]{2,1,0:T(8,128)(2,1)} %get-tuple-element.168.qT_ref, bf16[64,384]{1,0:T(8,128)(2,1)} %get-tuple-element.169.tab_ref, ...), custom_call_target="tpu_custom_call" | custom-call | flops 10737418240 | bytes 6144000 | tf_op jit(solution)/shard_map/attn_bwd/pallas_call | solution.py:318
  288.4 3.1 collective-permute-start.30
  291.5 15.1 %attn_bwd.8 = (bf16[192,512]{1,0:T(8,128)(2,1)}, bf16[192,512]{1,0:T(8,128)(2,1)}, bf16[192,512]{1,0:T(8,128)(2,1)}, bf16[192,512]{1,0:T(8,128)(2,1)}, f32[64,256]{1,0:T(8,128)}) custom-call(s32[3]{0:T(128)} %add_add_fusion.1.sc_ref, bf16[3,64,2048]{2,1,0:T(8,128)(2,1)} %get-tuple-element.168.qT_ref, bf16[64,384]{1,0:T(8,128)(2,1)} %get-tuple-element.169.tab_ref, ...), custom_call_target="tpu_custom_call" | custom-call | flops 10737418240 | bytes 6144000 | tf_op jit(solution)/shard_map/attn_bwd/pallas_call | solution.py:318
  310.3 3.1 collective-permute-start.33
  313.4 15.1 %attn_bwd.9 = (bf16[192,512]{1,0:T(8,128)(2,1)}, bf16[192,512]{1,0:T(8,128)(2,1)}, bf16[192,512]{1,0:T(8,128)(2,1)}, bf16[192,512]{1,0:T(8,128)(2,1)}, f32[64,256]{1,0:T(8,128)}) custom-call(s32[3]{0:T(128)} %add_add_fusion.1.sc_ref, bf16[3,64,2048]{2,1,0:T(8,128)(2,1)} %get-tuple-element.168.qT_ref, bf16[64,384]{1,0:T(8,128)(2,1)} %get-tuple-element.169.tab_ref, ...), custom_call_target="tpu_custom_call" | custom-call | flops 10737418240 | bytes 6144000 | tf_op jit(solution)/shard_map/attn_bwd/pallas_call | solution.py:318
  334.6 7.6 %qkv_weights.1 = (bf16[2,192,576]{2,1,0:T(8,128)(2,1)}, bf16[2,192,576]{2,1,0:T(8,128)(2,1)}, f32[3,192,128]{2,1,0:T(8,128)}, f32[8,768]{1,0:T(8,128)}) custom-call(s32[3]{0:T(128)} %add_add_fusion.1.sc_ref, bf16[4,512,768]{2,1,0:T(8,128)(2,1)} %bitcast.124, f32[8,768]{1,0:T(8,128)} %get-tuple-element.167.v_ref, bf16[576,768]{1,0:T(8,128)(2,1)} %get-tuple-element.256.wt_ref, ...), custom_call_target="tpu_custom_call" | custom-call | flops 1811939328 | bytes 8388608 | tf_op jit(solution)/shard_map/qkv_weights/pallas_call | solution.py:361
  344.9 18.9 %collective-permute-done.35.rest_10_ = bf16[192,512]{1,0:T(8,128)(2,1)S(1)} collective-permute-done((bf16[192,512]{1,0:T(8,128)(2,1)}, bf16[192,512]{1,0:T(8,128)(2,1)S(1)}, u32[]{:S(2)}, u32[]{:S(2)}) %collective-permute-start.35) | collective-permute-done | bytes 196640 | tf_op jit(solution)/shard_map/ppermute | solution.py:716
  363.8 4.1 collective-permute-start.37
  370.4 8.8 %norm1_grad.1 = bf16[512,768]{1,0:T(8,128)(2,1)} custom-call(s32[3]{0:T(128)} %add_add_fusion.1.sc_ref, bf16[2048,768]{1,0:T(8,128)(2,1)} %bitcast.95, f32[512,768]{1,0:T(8,128)} %get-tuple-element.200.dy_ref, f32[8,768]{1,0:T(8,128)} %get-tuple-element.167.v_ref, bf16[192,512]{1,0:T(8,128)(2,1)} %get-tuple-element.274.rest_0_, bf16[192,512]{1,0:T(8,128)(2,1)} %copy-done.5, ...), custom_call_target="tpu_custom_call" | custom-call | flops 1811939328 | bytes 8388608 | tf_op jit(solution)/shard_map/norm1_grad/pallas_call | solution.py:361
  381.5 4.9 %collective-permute-done.41 = f32[100,256]{1,0:T(8,128)S(1)} collective-permute-done((f32[100,256]{1,0:T(8,128)S(1)}, f32[100,256]{1,0:T(8,128)S(1)}, u32[]{:S(2)}, u32[]{:S(2)}) %collective-permute-start.41) | collective-permute-done | bytes 102432 | tf_op jit(solution)/shard_map/ppermute | solution.py:716
  386.6 5.0 %copied.1 = bf16[2048,768]{1,0:T(8,128)(2,1)} custom-call(s32[3]{0:T(128)} %add_add_fusion.1.sc_ref, bf16[2048,768]{1,0:T(8,128)(2,1)} %all-gather.18.cloned.1.call-done), custom_call_target="tpu_custom_call" | custom-call | bytes 4194304 | tf_op jit(solution)/shard_map/copied/pallas_call | solution.py:361
  394.8 4.2 collective-permute-done.44
  402.0 6.1 %collective-permute-done.45 = bf16[192,576]{1,0:T(8,128)(2,1)S(1)} collective-permute-done((bf16[192,576]{1,0:T(8,128)(2,1)S(1)}, bf16[192,576]{1,0:T(8,128)(2,1)S(1)}, u32[]{:S(2)}, u32[]{:S(2)}) %collective-permute-start.45) | collective-permute-done | bytes 221216 | tf_op jit(solution)/shard_map/ppermute | solution.py:716
  408.4 4.5 collective-permute-done.46
  414.1 25.9 %all-gather.10.cloned.1.call-done = bf16[2048,768]{1,0:T(8,128)(2,1)} async-done(((bf16[512,768]{1,0:T(8,128)(2,1)}), bf16[2048,768]{1,0:T(8,128)(2,1)}) %all-gather.10.cloned.1.call-update) | async-done | bytes 3145744 | tf_op jit(solution)/shard_map/all_gather | solution.py:893
  440.0 5.1 %bitcast_convert_fusion = f32[1,2048,768]{2,1,0:T(8,128)} fusion(bf16[2048,768]{1,0:T(8,128)(2,1)} %all-gather.10.cloned.1.call-done), kind=kLoop, calls=%fused_computation.2 | loop fusion | flops 1572864 | bytes 9437184 | tf_op jit(solution)/shard_map/reshape | solution.py:933
  (250 shorter events, 78.3 us)
Async XLA Ops:
  7.2 133.9 %all-gather.12.cloned.1.call-start = ((), (), s32[]{:S(2)}) async-start(), calls=%async_computation.3 | async-start | bytes 5013504 | tf_op jit(solution)/shard_map/all_gather | solution.py:725
  7.9 146.5 %all-gather.14.cloned.1.call-start = ((), (), s32[]{:S(2)}) async-start(), calls=%async_computation.4 | async-start | bytes 5013504 | tf_op jit(solution)/shard_map/all_gather | solution.py:725
  8.7 197.9 %all-gather.16.cloned.1.call-start = ((), (), s32[]{:S(2)}) async-start(), calls=%async_computation.5 | async-start | bytes 4177920 | tf_op jit(solution)/shard_map/all_gather | solution.py:725
  31.7 38.6 %collective-permute-start.6 = (bf16[2,208,192]{2,1,0:T(8,128)(2,1)S(1)}, bf16[2,208,192]{2,1,0:T(8,128)(2,1)S(1)}, u32[]{:S(2)}, u32[]{:S(2)}) collective-permute-start(bf16[2,208,192]{2,1,0:T(8,128)(2,1)S(1)} %pad_maximum_fusion.3), channel_id=1, source_target_pairs={{0,2},{1,3},{2,0},{3,1},{4,6},{5,7},{6,4},{7,5},{8,10},{9,11},{10,... | collective-permute-start | bytes 479240 | tf_op jit(solution)/shard_map/ppermute | solution.py:716
  43.3 29.0 %collective-permute-start.4 = (bf16[128,2048]{1,0:T(8,128)(2,1)}, bf16[128,2048]{1,0:T(8,128)(2,1)S(1)}, u32[]{:S(2)}, u32[]{:S(2)}) collective-permute-start(bf16[128,2048]{1,0:T(8,128)(2,1)} %get-tuple-element.170.rest_0_), channel_id=1, source_target_pairs={{0,4},{4,0},{1,5},{5,1},{2,6},{6,2},{3,7},{7,3},{8,12},{12,8},{9,1... | collective-permute-start | bytes 1572872 | tf_op jit(solution)/shard_map/ppermute | solution.py:711
  44.8 27.5 %collective-permute-start.5 = (bf16[128,2048]{1,0:T(8,128)(2,1)}, bf16[128,2048]{1,0:T(8,128)(2,1)S(1)}, u32[]{:S(2)}, u32[]{:S(2)}) collective-permute-start(bf16[128,2048]{1,0:T(8,128)(2,1)} %get-tuple-element.171.rest_1_.rest_0_), channel_id=1, source_target_pairs={{0,4},{4,0},{1,5},{5,1},{2,6},{6,2},{3,7},{7,3},{8,12},{12,8},{9,1... | collective-permute-start | bytes 1572872 | tf_op jit(solution)/shard_map/ppermute | solution.py:711
  45.3 49.1 %collective-permute-start.10 = (bf16[128,2048]{1,0:T(8,128)(2,1)}, bf16[128,2048]{1,0:T(8,128)(2,1)S(1)}, u32[]{:S(2)}, u32[]{:S(2)}) collective-permute-start(bf16[128,2048]{1,0:T(8,128)(2,1)} %get-tuple-element.172.rest_2_.rest_0_), channel_id=1, source_target_pairs={{0,4},{4,0},{1,5},{5,1},{2,6},{6,2},{3,7},{7,3},{8,12},{12,8},{9,1... | collective-permute-start | bytes 1572872 | tf_op jit(solution)/shard_map/ppermute | solution.py:711
  70.5 23.3 %collective-permute-start.11 = (bf16[4,208,192]{2,1,0:T(8,128)(2,1)S(1)}, bf16[4,208,192]{2,1,0:T(8,128)(2,1)S(1)}, u32[]{:S(2)}, u32[]{:S(2)}) collective-permute-start(bf16[4,208,192]{2,1,0:T(8,128)(2,1)S(1)} %pad_maximum_fusion.2.rest_8_), channel_id=1, source_target_pairs={{0,16},{8,24},{16,0},{24,8},{1,17},{9,25},{17,1},{25,9},{2,18},{10... | collective-permute-start | bytes 958472 | tf_op jit(solution)/shard_map/ppermute | solution.py:716
  72.3 35.2 %collective-permute-start.12 = (bf16[4,208,192]{2,1,0:T(8,128)(2,1)S(1)}, bf16[4,208,192]{2,1,0:T(8,128)(2,1)S(1)}, u32[]{:S(2)}, u32[]{:S(2)}) collective-permute-start(bf16[4,208,192]{2,1,0:T(8,128)(2,1)S(1)} %pad_maximum_fusion.2.rest_8_), channel_id=1, source_target_pairs={{0,8},{8,0},{16,24},{24,16},{1,9},{9,1},{17,25},{25,17},{2,10},{10... | collective-permute-start | bytes 958472 | tf_op jit(solution)/shard_map/ppermute | solution.py:716
  93.8 23.6 %collective-permute-start.13 = (bf16[4,208,192]{2,1,0:T(8,128)(2,1)S(1)}, bf16[4,208,192]{2,1,0:T(8,128)(2,1)S(1)}, u32[]{:S(2)}, u32[]{:S(2)}) collective-permute-start(bf16[4,208,192]{2,1,0:T(8,128)(2,1)S(1)} %collective-permute-done.11.rest_10_), channel_id=1, source_target_pairs={{0,8},{8,0},{16,24},{24,16},{1,9},{9,1},{17,25},{25,17},{2,10},{10... | collective-permute-start | bytes 958472 | tf_op jit(solution)/shard_map/ppermute | solution.py:716
  107.0 33.1 %collective-permute-start.7 = (bf16[128,512]{1,0:T(8,128)(2,1)S(1)}, bf16[128,512]{1,0:T(8,128)(2,1)S(1)}, u32[]{:S(2)}, u32[]{:S(2)}) collective-permute-start(bf16[128,512]{1,0:T(8,128)(2,1)S(1)} %copy-done.38), channel_id=1, source_target_pairs={{0,1},{1,0},{2,3},{3,2},{4,5},{5,4},{6,7},{7,6},{8,9},{9,8},{10,11... | collective-permute-start | bytes 393224 | tf_op jit(solution)/shard_map/ppermute | solution.py:716
  107.4 32.7 %collective-permute-start.8 = (bf16[128,512]{1,0:T(8,128)(2,1)S(1)}, bf16[128,512]{1,0:T(8,128)(2,1)S(1)}, u32[]{:S(2)}, u32[]{:S(2)}) collective-permute-start(bf16[128,512]{1,0:T(8,128)(2,1)S(1)} %copy-done.37), channel_id=1, source_target_pairs={{0,2},{1,3},{2,0},{3,1},{4,6},{5,7},{6,4},{7,5},{8,10},{9,11},{10,... | collective-permute-start | bytes 393224 | tf_op jit(solution)/shard_map/ppermute | solution.py:716
  107.5 32.6 %collective-permute-start.9 = (bf16[128,512]{1,0:T(8,128)(2,1)S(1)}, bf16[128,512]{1,0:T(8,128)(2,1)S(1)}, u32[]{:S(2)}, u32[]{:S(2)}) collective-permute-start(bf16[128,512]{1,0:T(8,128)(2,1)S(1)} %copy-done.36), channel_id=1, source_target_pairs={{0,3},{1,2},{2,1},{3,0},{4,7},{5,6},{6,5},{7,4},{8,11},{9,10},{10,... | collective-permute-start | bytes 393224 | tf_op jit(solution)/shard_map/ppermute | solution.py:716
  117.3 22.7 %collective-permute-start.15 = (bf16[64,512]{1,0:T(8,128)(2,1)}, bf16[64,512]{1,0:T(8,128)(2,1)S(1)}, u32[]{:S(2)}, u32[]{:S(2)}) collective-permute-start(bf16[64,512]{1,0:T(8,128)(2,1)} %get-tuple-element.191), channel_id=1, source_target_pairs={{0,2},{1,3},{2,0},{3,1},{4,6},{5,7},{6,4},{7,5},{8,10},{9,11},{10,... | collective-permute-start | bytes 196616 | tf_op jit(solution)/shard_map/ppermute | solution.py:716
  117.4 22.7 %collective-permute-start.16 = (bf16[64,512]{1,0:T(8,128)(2,1)}, bf16[64,512]{1,0:T(8,128)(2,1)S(1)}, u32[]{:S(2)}, u32[]{:S(2)}) collective-permute-start(bf16[64,512]{1,0:T(8,128)(2,1)} %get-tuple-element.192), channel_id=1, source_target_pairs={{0,3},{1,2},{2,1},{3,0},{4,7},{5,6},{6,5},{7,4},{8,11},{9,10},{10,... | collective-permute-start | bytes 196616 | tf_op jit(solution)/shard_map/ppermute | solution.py:716
  141.0 245.6 %all-gather.18.cloned.1.call-start = ((), (), s32[]{:S(2)}) async-start(), calls=%async_computation.6 | async-start | bytes 3932160 | tf_op jit(solution)/shard_map/all_gather | solution.py:851
  170.7 35.9 %collective-permute-start.17 = (bf16[192,512]{1,0:T(8,128)(2,1)}, bf16[192,512]{1,0:T(8,128)(2,1)S(1)}, u32[]{:S(2)}, u32[]{:S(2)}) collective-permute-start(bf16[192,512]{1,0:T(8,128)(2,1)} %get-tuple-element.208), channel_id=1, source_target_pairs={{0,1},{1,0},{2,3},{3,2},{4,5},{5,4},{6,7},{7,6},{8,9},{9,8},{10,11... | collective-permute-start | bytes 589832 | tf_op jit(solution)/shard_map/ppermute | solution.py:716
  172.3 34.3 %collective-permute-start.18 = (bf16[192,512]{1,0:T(8,128)(2,1)}, bf16[192,512]{1,0:T(8,128)(2,1)S(1)}, u32[]{:S(2)}, u32[]{:S(2)}) collective-permute-start(bf16[192,512]{1,0:T(8,128)(2,1)} %get-tuple-element.209), channel_id=1, source_target_pairs={{0,2},{1,3},{2,0},{3,1},{4,6},{5,7},{6,4},{7,5},{8,10},{9,11},{10,... | collective-permute-start | bytes 589832 | tf_op jit(solution)/shard_map/ppermute | solution.py:716
  172.4 34.2 %collective-permute-start.19 = (bf16[192,512]{1,0:T(8,128)(2,1)}, bf16[192,512]{1,0:T(8,128)(2,1)S(1)}, u32[]{:S(2)}, u32[]{:S(2)}) collective-permute-start(bf16[192,512]{1,0:T(8,128)(2,1)} %get-tuple-element.210), channel_id=1, source_target_pairs={{0,3},{1,2},{2,1},{3,0},{4,7},{5,6},{6,5},{7,4},{8,11},{9,10},{10,... | collective-permute-start | bytes 589832 | tf_op jit(solution)/shard_map/ppermute | solution.py:716
  192.1 31.7 %collective-permute-start.20 = (bf16[4,192,1728]{2,1,0:T(8,128)(2,1)}, bf16[4,192,1728]{2,1,0:T(8,128)(2,1)}, u32[]{:S(2)}, u32[]{:S(2)}) collective-permute-start(bf16[4,192,1728]{2,1,0:T(8,128)(2,1)} %get-tuple-element.219), channel_id=1, source_target_pairs={{0,8},{8,0},{16,24},{24,16},{1,9},{9,1},{17,25},{25,17},{2,10},{10... | collective-permute-start | bytes 7962632 | tf_op jit(solution)/shard_map/ppermute | solution.py:716
  192.1 31.6 %collective-permute-start.21 = (bf16[4,192,1728]{2,1,0:T(8,128)(2,1)}, bf16[4,192,1728]{2,1,0:T(8,128)(2,1)}, u32[]{:S(2)}, u32[]{:S(2)}) collective-permute-start(bf16[4,192,1728]{2,1,0:T(8,128)(2,1)} %get-tuple-element.220), channel_id=1, source_target_pairs={{0,8},{8,0},{16,24},{24,16},{1,9},{9,1},{17,25},{25,17},{2,10},{10... | collective-permute-start | bytes 7962632 | tf_op jit(solution)/shard_map/ppermute | solution.py:716
  222.2 49.6 %collective-permute-start.24 = (bf16[1,128,2048]{2,1,0:T(8,128)(2,1)}, bf16[1,128,2048]{2,1,0:T(8,128)(2,1)}, u32[]{:S(2)}, u32[]{:S(2)}) collective-permute-start(bf16[1,128,2048]{2,1,0:T(8,128)(2,1)} %get-tuple-element.230), channel_id=1, source_target_pairs={{0,4},{4,0},{1,5},{5,1},{2,6},{6,2},{3,7},{7,3},{8,12},{12,8},{9,1... | collective-permute-start | bytes 1572872 | tf_op jit(solution)/shard_map/ppermute | solution.py:711
  223.7 177.8 %reduce-scatter.2.cloned.1.call-start = ((), (), s32[]{:S(2)}) async-start(), calls=%async_computation.2 | async-start | bytes 1720320 | tf_op jit(solution)/shard_map/reduce_scatter | solution.py:877
  230.2 36.5 %collective-permute-start.23 = (bf16[4,96,1728]{2,1,0:T(8,128)(2,1)}, bf16[4,96,1728]{2,1,0:T(8,128)(2,1)S(1)}, u32[]{:S(2)}, u32[]{:S(2)}) collective-permute-start(bf16[4,96,1728]{2,1,0:T(8,128)(2,1)} %dynamic-slice_bitcast_fusion), channel_id=1, source_target_pairs={{0,4},{4,0},{1,5},{5,1},{2,6},{6,2},{3,7},{7,3},{8,12},{12,8},{9,1... | collective-permute-start | bytes 3981320 | tf_op jit(solution)/shard_map/ppermute | solution.py:716
  230.8 35.9 %collective-permute-start.22 = (bf16[2,192,1728]{2,1,0:T(8,128)(2,1)S(1)}, bf16[2,192,1728]{2,1,0:T(8,128)(2,1)}, u32[]{:S(2)}, u32[]{:S(2)}) collective-permute-start(bf16[2,192,1728]{2,1,0:T(8,128)(2,1)S(1)} %get-tuple-element.343), channel_id=1, source_target_pairs={{0,16},{8,24},{16,0},{24,8},{1,17},{9,25},{17,1},{25,9},{2,18},{10... | collective-permute-start | bytes 3981320 | tf_op jit(solution)/shard_map/ppermute | solution.py:716
  261.4 30.2 %collective-permute-start.26 = (bf16[2,128,2048]{2,1,0:T(8,128)(2,1)}, bf16[2,128,2048]{2,1,0:T(8,128)(2,1)}, u32[]{:S(2)}, u32[]{:S(2)}) collective-permute-start(bf16[2,128,2048]{2,1,0:T(8,128)(2,1)} %get-tuple-element.234), channel_id=1, source_target_pairs={{0,4},{4,0},{1,5},{5,1},{2,6},{6,2},{3,7},{7,3},{8,12},{12,8},{9,1... | collective-permute-start | bytes 3145736 | tf_op jit(solution)/shard_map/ppermute | solution.py:711
  268.4 38.3 %collective-permute-start.27 = (bf16[2,96,1728]{2,1,0:T(8,128)(2,1)S(1)}, bf16[2,96,1728]{2,1,0:T(8,128)(2,1)S(1)}, u32[]{:S(2)}, u32[]{:S(2)}) collective-permute-start(bf16[2,96,1728]{2,1,0:T(8,128)(2,1)S(1)} %dynamic-slice_bitcast_fusion.1), channel_id=1, source_target_pairs={{0,4},{4,0},{1,5},{5,1},{2,6},{6,2},{3,7},{7,3},{8,12},{12,8},{9,1... | collective-permute-start | bytes 1990664 | tf_op jit(solution)/shard_map/ppermute | solution.py:716
  308.4 131.7 %all-gather.10.cloned.1.call-start = ((), (), s32[]{:S(2)}) async-start(), calls=%async_computation.1 | async-start | bytes 3932160 | tf_op jit(solution)/shard_map/all_gather | solution.py:893
  309.0 25.5 %collective-permute-start.32 = (bf16[192,512]{1,0:T(8,128)(2,1)S(1)}, bf16[192,512]{1,0:T(8,128)(2,1)S(1)}, u32[]{:S(2)}, u32[]{:S(2)}) collective-permute-start(bf16[192,512]{1,0:T(8,128)(2,1)S(1)} %copy-done.31), channel_id=1, source_target_pairs={{0,2},{1,3},{2,0},{3,1},{4,6},{5,7},{6,4},{7,5},{8,10},{9,11},{10,... | collective-permute-start | bytes 589832 | tf_op jit(solution)/shard_map/ppermute | solution.py:716
  310.3 24.2 %collective-permute-start.33 = (bf16[192,512]{1,0:T(8,128)(2,1)S(1)}, bf16[192,512]{1,0:T(8,128)(2,1)S(1)}, u32[]{:S(2)}, u32[]{:S(2)}) collective-permute-start(bf16[192,512]{1,0:T(8,128)(2,1)S(1)} %copy-done.32), channel_id=1, source_target_pairs={{0,3},{1,2},{2,1},{3,0},{4,7},{5,6},{6,5},{7,4},{8,11},{9,10},{10,... | collective-permute-start | bytes 589832 | tf_op jit(solution)/shard_map/ppermute | solution.py:716
  328.7 35.1 %collective-permute-start.35 = (bf16[192,512]{1,0:T(8,128)(2,1)}, bf16[192,512]{1,0:T(8,128)(2,1)S(1)}, u32[]{:S(2)}, u32[]{:S(2)}) collective-permute-start(bf16[192,512]{1,0:T(8,128)(2,1)} %get-tuple-element.259.rest_10_), channel_id=1, source_target_pairs={{0,2},{1,3},{2,0},{3,1},{4,6},{5,7},{6,4},{7,5},{8,10},{9,11},{10,... | collective-permute-start | bytes 589832 | tf_op jit(solution)/shard_map/ppermute | solution.py:716
  330.0 33.9 %collective-permute-start.36 = (bf16[192,512]{1,0:T(8,128)(2,1)}, bf16[192,512]{1,0:T(8,128)(2,1)S(1)}, u32[]{:S(2)}, u32[]{:S(2)}) collective-permute-start(bf16[192,512]{1,0:T(8,128)(2,1)} %get-tuple-element.260.rest_11_), channel_id=1, source_target_pairs={{0,3},{1,2},{2,1},{3,0},{4,7},{5,6},{6,5},{7,4},{8,11},{9,10},{10,... | collective-permute-start | bytes 589832 | tf_op jit(solution)/shard_map/ppermute | solution.py:716
  (63 other events, 727.3 us)
Sparse Core Ops, SparseCore 0:
  10.3 63.8 all-gather.11
  76.5 65.4 all-gather.13
  144.3 62.2 all-gather.15
  223.8 60.8 all-gather.17
  308.5 49.1 reduce-scatter.1
  379.3 60.6 all-gather.9
where the time goes:
time: 463 us; the launch traced here: 455 us
  Pallas kernels  222 us (48%)
  waiting for transfers between devices  126 us (27%)
  starting transfers between devices  59.4 us (13%)
  other arithmetic  16.2 us (3%)
  local copies, waits for them, and re-layouts  16 us (3%)
  between operations  15.2 us (3%)
    pallas_call x5, Pallas kernels, attn_bwd(): pl.pallas_call(functools.partial(bwd_kernel, R=R, bk=bk, has_dq=dq is not...  89.4 us
    ppermute x42, waiting for transfers between devices, flip(): return lax.ppermute(value, axis, [(s, s ^ bit) for s in range(n)])  84.3 us
    pallas_call x8, Pallas kernels, call(): pl.pallas_call(kernel, grid_spec=pltpu.PrefetchScalarGridSpec(num_scalar_...  79.2 us
    pallas_call x3, Pallas kernels, attn_fwd(): pl.pallas_call(functools.partial(fwd_kernel, R=R, bk=bk, first=first, las...  53.6 us
    ppermute x42, starting transfers between devices, flip(): return lax.ppermute(value, axis, [(s, s ^ bit) for s in range(n)])  52.2 us
    all_gather x1, waiting for transfers between devices, per_device(): gall = lax.all_gather(gin, 'tensor', axis=0, tiled=True)  25.9 us
    all_gather x3, waiting for transfers between devices, gather_weights(): lax.all_gather(shard, ('dp', 'tensor')).reshape((nd, nt) + shard.shape)  14 us
  transfers between devices with their start and end apart: 53, of which 15 were waited for; matrix products, arithmetic and copies ran while one was open for 5% of the time, Pallas kernels for 49%

commit v1 on v0

--- a/solution.py
+++ b/solution.py
@@ -444,9 +444,9 @@
 
 def mlpa_kernel(sc_ref, x_ref, v_ref, *rest, nt, fb):
     no = 2 * nt
-    os, ps, p1, rest = rest[:no], rest[no : no + 4], rest[no + 4], rest[no + 5 :]
-    a_ref, sl_ref, h2_ref, y1_ref, wt_ref, wp, b4, bias = rest
-    dd, ft = p1.shape[1:]
+    os, ps, p1, rest = rest[:no], rest[no : no + 4], rest[no + 4 : no + 8], rest[no + 8 :]
+    a_ref, sl_ref, h2_ref, y1_ref, wt_ref, wp, b4, bias, wi = rest
+    dd, ft = p1[0].shape
     D = 4 * dd
     k = pl.program_id(0)
 
@@ -465,6 +465,7 @@
         xh, _ = norm_parts(y)
         h2_ref[...] = (xh * v_ref[2:3, :] + v_ref[3:4, :]).astype(bf16)
 
+    assemble(sc_ref, wi, p1)
     for r in range(4):
         b4[sc_ref[2] ^ r] = ps[r][k, dd:, :].astype(f32)
     rows = jnp.concatenate([b4[j, :, 0:16] for j in range(4)], 1)
@@ -472,21 +473,31 @@
         bias[:, i * 64 : (i + 1) * 64] = rows[i : i + 1]
     for j in range(ft // fb):
         sl = slice(j * fb, (j + 1) * fb)
-        wi = p1[:, :, sl].reshape(D, fb)
-        u = jnp.dot(h2_ref[...], wi, preferred_element_type=f32) + bias[:, sl]
+        u = jnp.dot(h2_ref[...], wi[:, sl], preferred_element_type=f32) + bias[:, sl]
         cdf = 0.5 + 0.5 * lax.erf(u * 0.7071067811865476)
         a_ref[:, sl] = (u * cdf).astype(bf16)
         slope = cdf + u * (jnp.exp(-0.5 * u * u) * 0.3989422804014327)
         sl_ref[:, sl] = slope.astype(sl_ref.dtype)
 
 
-def back_block(nd, rows, cols):
-    return pl.BlockSpec((nd, None, rows, cols), lambda k, s: (0, s[1] ^ k, 0, 0))
+def piece_specs(w):
+    n2, dd, cols = w[0].shape
+    at = lambda add: pl.BlockSpec((None, dd, cols), lambda k, s: (add + (s[1] ^ k), 0, 0))
+    return [at(0), at(0), at(n2 // 2), at(n2 // 2)]
+
+
+def pieces(w):
+    return [w[0], w[1], w[0], w[1]]
+
+
+def assemble(sc_ref, whole, parts):
+    for r, p in enumerate(parts):
+        whole[rows_of(sc_ref, r, p.shape[0]), :] = p[...]
 
 
 def mlpa(sc, x, vecs, os, ps, p1):
     D = x.shape[1]
-    nd, nt, dd, ft = p1.shape
+    nt, ft = ps[0].shape[0], p1[0].shape[2]
     N = os[0].shape[1]
     kt = ps[0].shape[2]
     mine = pl.BlockSpec((N, D), lambda k, s: (s[1], 0))
@@ -497,32 +508,36 @@
         [mine, whole_spec(vecs.shape)]
         + [whole_spec(o.shape) for o in os]
         + [whole_spec(p.shape) for p in ps]
-        + [back_block(nd, dd, ft)],
-        [x, vecs, *os, *ps, p1],
+        + piece_specs(p1),
+        [x, vecs, *os, *ps, *pieces(p1)],
         [act, act, full, full, whole_spec((nt, kt, D))],
         [((nt, N, ft), bf16), ((nt, N, ft), f32), ((N, D), bf16), ((N, D), f32)]
         + [((nt, kt, D), bf16)],
-        [pltpu.VMEM((D, kt), bf16), pltpu.VMEM((4, 16, kt), f32), pltpu.VMEM((1, ft), f32)],
+        [pltpu.VMEM((D, kt), bf16), pltpu.VMEM((4, 16, kt), f32), pltpu.VMEM((1, ft), f32)]
+        + [pltpu.VMEM((D, ft), bf16)],
         "mlp_in", 3 * N * D * ft * nt, 24 * 2**20,
     )
 
 
 def mlpb_kernel(sc_ref, g_ref, v_ref, y1_ref, sl_ref, *rest, nt, fb):
-    wt_ref, p1, p2, du_ref, da_ref, dy_ref, sm_ref, db_ref, *dos, dh = rest
-    D, ft = p1.shape[0] * p1.shape[1], p1.shape[2]
+    wt_ref, p1, p2, rest = rest[0], rest[1:5], rest[5:9], rest[9:]
+    du_ref, da_ref, dy_ref, sm_ref, db_ref, *dos, dh, wi, wo = rest
+    D, ft = wi.shape
     k = pl.program_id(0)
 
     @pl.when(k == 0)
     def _():
         dh[...] = jnp.zeros_like(dh)
 
+    assemble(sc_ref, wo, p2)
+    assemble(sc_ref, wi, p1)
     for j in range(ft // fb):
         sl = slice(j * fb, (j + 1) * fb)
-        ga = jnp.dot(g_ref[...], p2[:, :, sl].reshape(D, fb), preferred_element_type=f32)
+        ga = jnp.dot(g_ref[...], wo[:, sl], preferred_element_type=f32)
         du = (sl_ref[:, sl] * ga).astype(bf16)
         du_ref[:, sl] = du
         db_ref[:, sl] = jnp.sum(du.astype(f32), axis=0, keepdims=True)
-        dh[...] += dot(du, p1[:, :, sl].reshape(D, fb), 1, 1)
+        dh[...] += dot(du, wi[:, sl], 1, 1)
 
     @pl.when(k == pl.num_programs(0) - 1)
     def _():
@@ -541,8 +556,8 @@
 
 def mlpb(sc, g, vecs, y1, slope, wt, p1, p2):
     N, D = y1.shape
-    nd, nt, dd, ft = p1.shape
-    kt = wt.shape[1]
+    nt, kt = wt.shape[:2]
+    ft = p1[0].shape[2]
     act = pl.BlockSpec((None, N, ft), lambda k, s: (k, 0, 0))
     row = pl.BlockSpec((None, 1, ft), lambda k, s: (s[1] ^ k, 0, 0))
     full = whole_spec((N, D))
@@ -550,20 +565,21 @@
         functools.partial(mlpb_kernel, nt=nt, fb=256), sc, (nt,),
         [pl.BlockSpec((N, D), lambda k, s: (s[1], 0)), whole_spec(vecs.shape), full, act]
         + [whole_spec(wt.shape)]
-        + [back_block(nd, dd, ft)] * 2,
-        [g, vecs, y1, slope, wt, p1, p2],
+        + piece_specs(p1)
+        + piece_specs(p2),
+        [g, vecs, y1, slope, wt, *pieces(p1), *pieces(p2)],
         [act, full, full, whole_spec((8, D)), row] + [whole_spec((kt, N))] * nt,
         [((nt, N, ft), bf16), ((N, D), bf16), ((N, D), f32), ((8, D), f32), ((nt, 1, ft), f32)]
         + [((kt, N), bf16)] * nt,
-        [pltpu.VMEM((N, D), f32)],
+        [pltpu.VMEM((N, D), f32)] + [pltpu.VMEM((D, ft), bf16)] * 2,
         "mlp_grad", 5 * N * D * ft * nt, 24 * 2**20,
     )
 
 
 def mlp2_kernel(sc_ref, g_ref, v_ref, h2_ref, da_ref, y_ref, a_ref, du_ref, *rest, nt):
     no = 2 * nt
-    os, (p2, *rest) = rest[:no], rest[no:]
-    gws, (out_ref, hT, gT, dT, oa, acc, acn) = rest[:4], rest[4:]
+    os, p2, rest = rest[:no], rest[no : no + 4], rest[no + 4 :]
+    gws, (out_ref, hT, gT, dT, oa, acc, acn, wo) = rest[:4], rest[4:]
     ft = a_ref.shape[1]
     D = h2_ref.shape[1]
     dd = D // 4
@@ -582,7 +598,8 @@
         acc[...] = jnp.zeros_like(acc)
 
     a = a_ref[...]
-    acc[...] += dot(a, p2[...].reshape(D, ft), 1, 1)
+    assemble(sc_ref, wo, p2)
+    acc[...] += dot(a, wo[...], 1, 1)
 
     def store(value, lo, hi):
         value = value.astype(bf16)
@@ -600,7 +617,8 @@
 
 def mlp2(sc, g, vecs, h2, da, y1, a, du, os, p2):
     N, D = h2.shape
-    nd, nt, dd, ft = p2.shape
+    nt, _, ft = a.shape
+    dd = D // 4
     kt = os[0].shape[0] + os[nt].shape[0]
     cols = 2 * ft + kt
     full = whole_spec((N, D))
@@ -611,12 +629,17 @@
         [pl.BlockSpec((N, D), lambda k, s: (s[1], 0)), whole_spec(vecs.shape), full, full, full]
         + [act, act]
         + [whole_spec(o.shape) for o in os]
-        + [back_block(nd, dd, ft)],
-        [g, vecs, h2, da, y1, a, du, *os, p2],
+        + piece_specs(p2),
+        [g, vecs, h2, da, y1, a, du, *os, *pieces(p2)],
         [gw] * 4 + [full],
         [((nt, dd, cols), bf16)] * 4 + [((N, D), bf16)],
         [pltpu.VMEM((D, N), bf16)] * 3
-        + [pltpu.VMEM((nt, kt, N), bf16), pltpu.VMEM((N, D), f32), pltpu.VMEM((D, N), f32)],
+        + [
+            pltpu.VMEM((nt, kt, N), bf16),
+            pltpu.VMEM((N, D), f32),
+            pltpu.VMEM((D, N), f32),
+            pltpu.VMEM((D, ft), bf16),
+        ],
         "mlp_weights", 7 * N * D * ft * nt, 24 * 2**20,
     )
 
@@ -781,8 +804,8 @@
         pack_kernel, sc, (1,), [whole_spec(v.shape) for v in smalls], smalls,
         [whole_spec((dd + 32, 3 * E))], [((dd + 32, 3 * E), bf16)], [], "pack", 0, 2**16,
     )[0]
-    p1 = gather_weights(mlp_in_weight)
-    p2 = gather_weights(mlp_out_weight.T)
+    p1 = lax.all_gather(mlp_in_weight, "tensor", axis=0)
+    p2 = lax.all_gather(mlp_out_weight.T, "tensor", axis=0)
     brow = jnp.pad(mlp_in_bias, ((0, 16 - mlp_in_bias.shape[0]), (0, E - 16)))
     own = jnp.concatenate([proj_weight.T, brow], 0)
     near = flip(own, "tensor", 1)
@@ -796,7 +819,8 @@
     kv_far = [[shift(kv, "ctx", k) for kv in kvs] for k in range(1, nc)]
 
     state = attn_fwd(sc, 0, qT, kvs, tab, None, False, R, nt)
-    state, two = bar((state, two))
+    state, two, p1 = bar((state, two, p1))
+    p1x = flip(p1, "dp", 2)
     own = jnp.concatenate([own, two])
     far = flip(own, "dp", 2)
     for k in range(1, nc - 1):
@@ -807,12 +831,18 @@
             scalars(nc - 1), h0, qT, kv_far[-1][h0:h1], tab, state, True, R, nt
         )
         if h0 == 0:
-            state, far = bar((state, far))
+            state, far, p2 = bar((state, far, p2))
+            p2x = flip(p2, "dp", 2)
             ps = [own, flip(own, "dp", 1), far, flip(far, "dp", 1)]
         else:
-            o0, ps = bar((o0, ps))
+            o0, ps, p1, p1x, os = bar((o0, ps, p1, p1x, os))
+            p1 = jnp.concatenate([p1, p1x])
+            p1 = (p1, flip(p1, "dp", 1))
         os += spread([o0, o1, o2, o3])
     o32, lse = state
+    os, p2x = bar((os, p2x))
+    p2 = jnp.concatenate([p2, p2x])
+    p2 = (p2, flip(p2, "dp", 1))
     p3 = gather_weights(after(small[0], *os)[:dd])
     a, slope, h2, y1, wt = mlpa(sc, x2, vecs, os, ps, p1)
     du, da, dy1, sm2, dbin, *dos = mlpb(sc, g2, vecs, y1, slope, wt, p1, p2)
@@ -870,7 +900,7 @@
             if halves:
                 dtab, ya = bar((dtab, ya))
                 v = jnp.concatenate([add(part(va, pos), ya), add(vb[: nt // 2], xb)])
-            dtab, dxr, v = bar((dtab, dxr, v))
+            dtab, dxr, v, block_out = bar((dtab, dxr, v, block_out))
         if h == 2:
             dtab, dxr, xh1 = bar((dtab, dxr, xh1))
         dxr = dxr + spread(d)

time: 463 us -> 455 us (0.983)
  waiting for transfers between devices: 126 us -> 89.8 us
  starting transfers between devices: 59.4 us -> 77.1 us
  local copies, waits for them, and re-layouts: 16 us -> 23.3 us
    ppermute x42 -> x46, waiting for transfers between devices: 84.3 us -> 46.8 us  [flip(): return lax.ppermute(value, axis, [(s, s ^ bit) for s in range(n)])]
    ppermute x42 -> x46, starting transfers between devices: 52.2 us -> 71 us  [flip(): return lax.ppermute(value, axis, [(s, s ^ bit) for s in range(n)])]
    ppermute x5, waiting for transfers between devices: 0.01 us -> 15.1 us  [shift(): return lax.ppermute(value, axis, [(s, (s + steps) % n) for s in range(n)])]
    all_gather x3 -> x1, waiting for transfers between devices: 14 us -> 0.02 us  [gather_weights(): lax.all_gather(shard, ('dp', 'tensor')).reshape((nd, nt) + shard.shape)]
    unnamed x90 -> x102, local copies, waits for them, and re-layouts: 7.38 us -> 11.1 us
  transfers between devices with their start and end apart: 53 -> 57, of which waited for: 15 -> 20; matrix products, arithmetic and copies ran while one was open for 5% -> 4% of each run, Pallas kernels for 49% -> 50%
where the time goes in v1:
time: 455 us; the launch traced here: 446 us
  Pallas kernels  224 us (49%)
  waiting for transfers between devices  89.8 us (20%)
  starting transfers between devices  77.1 us (17%)
  local copies, waits for them, and re-layouts  23.3 us (5%)
  other arithmetic  16.7 us (4%)
  between operations  15.5 us (3%)
    pallas_call x5, Pallas kernels, attn_bwd(): pl.pallas_call(functools.partial(bwd_kernel, R=R, bk=bk, has_dq=dq is not...  89.8 us
    pallas_call x8, Pallas kernels, call(): pl.pallas_call(kernel, grid_spec=pltpu.PrefetchScalarGridSpec(num_scalar_...  81 us
    ppermute x46, starting transfers between devices, flip(): return lax.ppermute(value, axis, [(s, s ^ bit) for s in range(n)])  71 us
    pallas_call x3, Pallas kernels, attn_fwd(): pl.pallas_call(functools.partial(fwd_kernel, R=R, bk=bk, first=first, las...  53.1 us
    ppermute x46, waiting for transfers between devices, flip(): return lax.ppermute(value, axis, [(s, s ^ bit) for s in range(n)])  46.8 us
    all_gather x1, waiting for transfers between devices, per_device(): gall = lax.all_gather(gin, 'tensor', axis=0, tiled=True)  27 us
    ppermute x5, waiting for transfers between devices, shift(): return lax.ppermute(value, axis, [(s, (s + steps) % n) for s in range(n)])  15.1 us
    unnamed x102, local copies, waits for them, and re-layouts  11.1 us
  transfers between devices with their start and end apart: 57, of which 20 were waited for; matrix products, arithmetic and copies ran while one was open for 4% of the time, Pallas kernels for 50%

profile of v1, /device:TPU:0, one launch (start us, length us, event | category | flops | bytes accessed | tf_op | source)
XLA Modules:
  0.0 446.2 jit_solution(2253204595134708239)
XLA Ops:
  22.0 5.8 %collective-permute-done.3.s3 = bf16[224,576]{1,0:T(8,128)(2,1)S(1)} collective-permute-done((bf16[224,576]{1,0:T(8,128)(2,1)}, bf16[224,576]{1,0:T(8,128)(2,1)S(1)}, u32[]{:S(2)}, u32[]{:S(2)}) %collective-permute-start.3) | collective-permute-done | bytes 258080 | tf_op jit(solution)/shard_map/ppermute | solution.py:739
  30.5 8.8 %front.1 = (bf16[64,384]{1,0:T(8,128)(2,1)}, f32[8,768]{1,0:T(8,128)}, bf16[3,64,2048]{2,1,0:T(8,128)(2,1)}, bf16[128,2048]{1,0:T(8,128)(2,1)}, bf16[128,2048]{1...) custom-call(s32[3]{0:T(128)} %add_add_fusion.1.sc_ref, ...), custom_call_target="tpu_custom_call" | custom-call | flops 1811939328 | bytes 9437184 | tf_op jit(solution)/shard_map/front/pallas_call | solution.py:361
  41.4 23.3 %attn_fwd.3 = (f32[3,64,2048]{2,1,0:T(8,128)}, f32[3,8,2048]{2,1,0:T(8,128)}) custom-call(s32[3]{0:T(128)} %add_add_fusion.1.sc_ref, bf16[3,64,2048]{2,1,0:T(8,128)(2,1)} %get-tuple-element.186.qT_ref, bf16[64,384]{1,0:T(8,128)(2,1)} %get-tuple-element.187.tab_ref, bf16[128,2048]{1,0:T(8,128)(2,1)} %get-tuple-element.189.rest_0_, ...), custom_call_target="tpu_custom_call" | custom-call | flops 12884901888 | bytes 7372800 | tf_op jit(solution)/shard_map/attn_fwd/pallas_call | solution.py:152
  67.7 19.6 %attn_fwd.4 = (f32[3,64,2048]{2,1,0:T(8,128)}, f32[3,8,2048]{2,1,0:T(8,128)}, bf16[128,512]{1,0:T(8,128)(2,1)}, bf16[128,512]{1,0:T(8,128)(2,1)}, bf16[128,512]{1,0:T(8,128)(2,1)}, /*index=5*/bf16[128,512]{1,0:T(8,128)(2,1)}) custom-call(s32[3]{0:T(128)} %add_add_fusion.2.sc_ref, ...), custom_call_target="tpu_custom_call", output_to_operand_aliasing={{0}: (5, {}), {1}: (6, {})} | custom-call | flops 8589934592 | bytes 4915200 | tf_op jit(solution)/shard_map/attn_fwd/pallas_call | solution.py:152
  92.7 9.1 %collective-permute-done.4.rest_0_.rest_1_ = bf16[128,2048]{1,0:T(8,128)(2,1)S(1)} collective-permute-done((bf16[128,2048]{1,0:T(8,128)(2,1)S(1)}, bf16[128,2048]{1,0:T(8,128)(2,1)S(1)}, u32[]{:S(2)}, u32[]{:S(2)}) %collective-permute-start.4) | collective-permute-done | bytes 524320 | tf_op jit(solution)/shard_map/ppermute | solution.py:734
  104.5 10.2 %attn_fwd.5 = (f32[3,64,2048]{2,1,0:T(8,128)}, f32[3,8,2048]{2,1,0:T(8,128)}, bf16[64,512]{1,0:T(8,128)(2,1)}, bf16[64,512]{1,0:T(8,128)(2,1)}, bf16[64,512]{1,0:T(8,128)(2,1)}, /*index=5*/bf16[64,512]{1,0:T(8,128)(2,1)}) custom-call(s32[3]{0:T(128)} %add_add_fusion.2.sc_ref, ...), custom_call_target="tpu_custom_call", output_to_operand_aliasing={{0}: (4, {}), {1}: (5, {})} | custom-call | flops 4294967296 | bytes 2457600 | tf_op jit(solution)/shard_map/attn_fwd/pallas_call | solution.py:152
  123.7 3.3 collective-permute-done.18
  134.0 13.6 %mlp_in.1 = (bf16[4,512,768]{2,1,0:T(8,128)(2,1)}, f32[4,512,768]{2,1,0:T(8,128)}, bf16[512,768]{1,0:T(8,128)(2,1)}, f32[512,768]{1,0:T(8,128)}, bf16[4,192,768]{2,1,0:T(8,128)(2,1)}) custom-call(s32[3]{0:T(128)} %add_add_fusion.1.sc_ref, bf16[2048,768]{1,0:T(8,128)(2,1)} %bitcast.88, f32[8,768]{1,0:T(8,128)} %get-tuple-element.185.v_ref, ...), custom_call_target="tpu_custom_call" | custom-call | flops 3623878656 | bytes 25165824 | tf_op jit(solution)/shard_map/mlp_in/pallas_call | solution.py:361
  147.6 16.9 %mlp_grad.1 = (bf16[4,512,768]{2,1,0:T(8,128)(2,1)}, bf16[512,768]{1,0:T(8,128)(2,1)}, f32[512,768]{1,0:T(8,128)}, f32[8,768]{1,0:T(8,128)}, f32[4,1,768]{2,1,0:...) custom-call(s32[3]{0:T(128)} %add_add_fusion.1.sc_ref, ...), custom_call_target="tpu_custom_call" | custom-call | flops 6039797760 | bytes 25165824 | tf_op jit(solution)/shard_map/mlp_grad/pallas_call | solution.py:361
  168.9 17.6 %mlp_weights.1 = (bf16[4,192,1728]{2,1,0:T(8,128)(2,1)}, bf16[4,192,1728]{2,1,0:T(8,128)(2,1)}, bf16[4,192,1728]{2,1,0:T(8,128)(2,1)}, bf16[4,192,1728]{2,1,0:T(8,128)(2,1)}, bf16[512,768]{1,0:T(8,128)(2,1)}) custom-call(s32[3]{0:T(128)} %add_add_fusion.1.sc_ref, bf16[2048,768]{1,0:T(8,128)(2,1)} %bitcast.96, f32[8,768]{1,0:T(8,128)} %get-tuple-element.185.v_ref, ...), custom_call_target="tpu_custom_call" | custom-call | flops 8455716864 | bytes 25165824 | tf_op jit(solution)/shard_map/mlp_weights/pallas_call | solution.py:361
  189.0 15.2 %attn_bwd.5 = (f32[1,64,2048]{2,1,0:T(8,128)}, bf16[1,128,2048]{2,1,0:T(8,128)(2,1)}, f32[64,256]{1,0:T(8,128)}) custom-call(s32[3]{0:T(128)} %add_add_fusion.2.sc_ref, bf16[3,64,2048]{2,1,0:T(8,128)(2,1)} %get-tuple-element.186.qT_ref, bf16[64,384]{1,0:T(8,128)(2,1)} %get-tuple-element.187.tab_ref, bf16[128,2048]{1,0:T(8,128)(2,1)} %collective-permute-done.5.rest_0_, ...), custom_call_target="tpu_custom_call" | custom-call | flops 214748364800 | bytes 6144000 | tf_op jit(solution)/shard_map/attn_bwd/pallas_call | solution.py:318
  204.2 3.9 add_convert_fusion
  214.6 29.2 %attn_bwd.6 = (f32[2,64,2048]{2,1,0:T(8,128)}, bf16[2,128,2048]{2,1,0:T(8,128)(2,1)}, f32[64,256]{1,0:T(8,128)}) custom-call(s32[3]{0:T(128)} %add_add_fusion.2.sc_ref, bf16[3,64,2048]{2,1,0:T(8,128)(2,1)} %get-tuple-element.186.qT_ref, bf16[64,384]{1,0:T(8,128)(2,1)} %get-tuple-element.187.tab_ref, bf16[128,2048]{1,0:T(8,128)(2,1)} %copy-done.34, ...), custom_call_target="tpu_custom_call" | custom-call | flops 21474836480 | bytes 12288000 | tf_op jit(solution)/shard_map/attn_bwd/pallas_call | solution.py:318
  250.8 5.6 %collective-permute-done.28.rest_9_ = bf16[1,128,2048]{2,1,0:T(8,128)(2,1)} collective-permute-done((bf16[1,128,2048]{2,1,0:T(8,128)(2,1)S(1)}, bf16[1,128,2048]{2,1,0:T(8,128)(2,1)}, u32[]{:S(2)}, u32[]{:S(2)}) %collective-permute-start.28) | collective-permute-done | bytes 524320 | tf_op jit(solution)/shard_map/ppermute | solution.py:734
  256.4 15.1 %attn_bwd.7 = (bf16[192,512]{1,0:T(8,128)(2,1)}, bf16[192,512]{1,0:T(8,128)(2,1)}, bf16[192,512]{1,0:T(8,128)(2,1)}, bf16[192,512]{1,0:T(8,128)(2,1)}, f32[64,256]{1,0:T(8,128)}) custom-call(s32[3]{0:T(128)} %add_add_fusion.1.sc_ref, bf16[3,64,2048]{2,1,0:T(8,128)(2,1)} %get-tuple-element.186.qT_ref, bf16[64,384]{1,0:T(8,128)(2,1)} %get-tuple-element.187.tab_ref, ...), custom_call_target="tpu_custom_call" | custom-call | flops 10737418240 | bytes 6144000 | tf_op jit(solution)/shard_map/attn_bwd/pallas_call | solution.py:318
  271.5 4.4 collective-permute-start.32
  278.9 15.2 %attn_bwd.8 = (bf16[192,512]{1,0:T(8,128)(2,1)}, bf16[192,512]{1,0:T(8,128)(2,1)}, bf16[192,512]{1,0:T(8,128)(2,1)}, bf16[192,512]{1,0:T(8,128)(2,1)}, f32[64,256]{1,0:T(8,128)}) custom-call(s32[3]{0:T(128)} %add_add_fusion.1.sc_ref, bf16[3,64,2048]{2,1,0:T(8,128)(2,1)} %get-tuple-element.186.qT_ref, bf16[64,384]{1,0:T(8,128)(2,1)} %get-tuple-element.187.tab_ref, ...), custom_call_target="tpu_custom_call" | custom-call | flops 10737418240 | bytes 6144000 | tf_op jit(solution)/shard_map/attn_bwd/pallas_call | solution.py:318
  296.1 4.3 collective-permute-start.35
  302.8 15.1 %attn_bwd.9 = (bf16[192,512]{1,0:T(8,128)(2,1)}, bf16[192,512]{1,0:T(8,128)(2,1)}, bf16[192,512]{1,0:T(8,128)(2,1)}, bf16[192,512]{1,0:T(8,128)(2,1)}, f32[64,256]{1,0:T(8,128)}) custom-call(s32[3]{0:T(128)} %add_add_fusion.1.sc_ref, bf16[3,64,2048]{2,1,0:T(8,128)(2,1)} %get-tuple-element.186.qT_ref, bf16[64,384]{1,0:T(8,128)(2,1)} %get-tuple-element.187.tab_ref, ...), custom_call_target="tpu_custom_call" | custom-call | flops 10737418240 | bytes 6144000 | tf_op jit(solution)/shard_map/attn_bwd/pallas_call | solution.py:318
  318.0 7.7 %collective-permute-done.36.rest_6_ = bf16[192,512]{1,0:T(8,128)(2,1)S(1)} collective-permute-done((bf16[192,512]{1,0:T(8,128)(2,1)S(1)}, bf16[192,512]{1,0:T(8,128)(2,1)S(1)}, u32[]{:S(2)}, u32[]{:S(2)}) %collective-permute-start.36) | collective-permute-done | bytes 196640 | tf_op jit(solution)/shard_map/ppermute | solution.py:739
  325.8 11.6 %collective-permute-start.38 = (bf16[192,512]{1,0:T(8,128)(2,1)}, bf16[192,512]{1,0:T(8,128)(2,1)S(1)}, u32[]{:S(2)}, u32[]{:S(2)}) collective-permute-start(bf16[192,512]{1,0:T(8,128)(2,1)} %get-tuple-element.294.rest_9_), channel_id=1, source_target_pairs={{0,1},{1,0},{2,3},{3,2},{4,5},{5,4},{6,7},{7,6},{8,9},{9,8},{10,11... | collective-permute-start | bytes 589832 | tf_op jit(solution)/shard_map/ppermute | solution.py:739
  339.7 7.6 %qkv_weights.1 = (bf16[2,192,576]{2,1,0:T(8,128)(2,1)}, bf16[2,192,576]{2,1,0:T(8,128)(2,1)}, f32[3,192,128]{2,1,0:T(8,128)}, f32[8,768]{1,0:T(8,128)}) custom-call(s32[3]{0:T(128)} %add_add_fusion.1.sc_ref, bf16[4,512,768]{2,1,0:T(8,128)(2,1)} %bitcast.124, f32[8,768]{1,0:T(8,128)} %get-tuple-element.185.v_ref, bf16[576,768]{1,0:T(8,128)(2,1)} %get-tuple-element.292.wt_ref, ...), custom_call_target="tpu_custom_call" | custom-call | flops 1811939328 | bytes 8388608 | tf_op jit(solution)/shard_map/qkv_weights/pallas_call | solution.py:361
  350.1 2.8 collective-permute-done.39.rest_10_
  352.9 4.4 collective-permute-start.41
  359.7 8.9 %norm1_grad.1 = bf16[512,768]{1,0:T(8,128)(2,1)} custom-call(s32[3]{0:T(128)} %add_add_fusion.1.sc_ref, bf16[2048,768]{1,0:T(8,128)(2,1)} %bitcast.89, f32[512,768]{1,0:T(8,128)} %get-tuple-element.235.dy_ref, f32[8,768]{1,0:T(8,128)} %get-tuple-element.185.v_ref, bf16[192,512]{1,0:T(8,128)(2,1)} %get-tuple-element.310.rest_0_, bf16[192,512]{1,0:T(8,128)(2,1)} %copy-done.16, ...), custom_call_target="tpu_custom_call" | custom-call | flops 1811939328 | bytes 8388608 | tf_op jit(solution)/shard_map/norm1_grad/pallas_call | solution.py:361
  372.2 3.6 collective-permute-done.45
  377.3 5.0 %copied.1 = bf16[2048,768]{1,0:T(8,128)(2,1)} custom-call(s32[3]{0:T(128)} %add_add_fusion.1.sc_ref, bf16[2048,768]{1,0:T(8,128)(2,1)} %all-gather.18.cloned.1.call-done), custom_call_target="tpu_custom_call" | custom-call | bytes 4194304 | tf_op jit(solution)/shard_map/copied/pallas_call | solution.py:361
  386.2 3.3 collective-permute-done.48
  392.5 6.1 %collective-permute-done.49 = bf16[192,576]{1,0:T(8,128)(2,1)S(1)} collective-permute-done((bf16[192,576]{1,0:T(8,128)(2,1)S(1)}, bf16[192,576]{1,0:T(8,128)(2,1)S(1)}, u32[]{:S(2)}, u32[]{:S(2)}) %collective-permute-start.49) | collective-permute-done | bytes 221216 | tf_op jit(solution)/shard_map/ppermute | solution.py:739
  398.9 4.3 collective-permute-done.50
  404.4 27.0 %all-gather.10.cloned.1.call-done = bf16[2048,768]{1,0:T(8,128)(2,1)} async-done(((bf16[512,768]{1,0:T(8,128)(2,1)}), bf16[2048,768]{1,0:T(8,128)(2,1)}) %all-gather.10.cloned.1.call-update) | async-done | bytes 3145744 | tf_op jit(solution)/shard_map/all_gather | solution.py:923
  431.4 5.1 %bitcast_convert_fusion = f32[1,2048,768]{2,1,0:T(8,128)} fusion(bf16[2048,768]{1,0:T(8,128)(2,1)} %all-gather.10.cloned.1.call-done), kind=kLoop, calls=%fused_computation.2 | loop fusion | flops 1572864 | bytes 9437184 | tf_op jit(solution)/shard_map/reshape | solution.py:963
  (272 shorter events, 97.2 us)
Async XLA Ops:
  7.2 57.5 %all-gather.12.cloned.1.call-start = ((), (), s32[]{:S(2)}) async-start(), calls=%async_computation.3 | async-start | bytes 1474560 | tf_op jit(solution)/shard_map/all_gather | solution.py:807
  7.9 79.5 %all-gather.14.cloned.1.call-start = ((), (), s32[]{:S(2)}) async-start(), calls=%async_computation.4 | async-start | bytes 1474560 | tf_op jit(solution)/shard_map/all_gather | solution.py:808
  17.8 170.4 %all-gather.16.cloned.1.call-start = ((), (), s32[]{:S(2)}) async-start(), calls=%async_computation.5 | async-start | bytes 4177920 | tf_op jit(solution)/shard_map/all_gather | solution.py:748
  27.8 36.8 %collective-permute-start.7 = (bf16[2,208,192]{2,1,0:T(8,128)(2,1)S(1)}, bf16[2,208,192]{2,1,0:T(8,128)(2,1)S(1)}, u32[]{:S(2)}, u32[]{:S(2)}) collective-permute-start(bf16[2,208,192]{2,1,0:T(8,128)(2,1)S(1)} %pad_maximum_fusion.3), channel_id=1, source_target_pairs={{0,2},{1,3},{2,0},{3,1},{4,6},{5,7},{6,4},{7,5},{8,10},{9,11},{10,... | collective-permute-start | bytes 479240 | tf_op jit(solution)/shard_map/ppermute | solution.py:739
  39.4 27.6 %collective-permute-start.5 = (bf16[128,2048]{1,0:T(8,128)(2,1)}, bf16[128,2048]{1,0:T(8,128)(2,1)}, u32[]{:S(2)}, u32[]{:S(2)}) collective-permute-start(bf16[128,2048]{1,0:T(8,128)(2,1)} %get-tuple-element.189.rest_0_), channel_id=1, source_target_pairs={{0,4},{4,0},{1,5},{5,1},{2,6},{6,2},{3,7},{7,3},{8,12},{12,8},{9,1... | collective-permute-start | bytes 1572872 | tf_op jit(solution)/shard_map/ppermute | solution.py:734
  40.9 26.0 %collective-permute-start.6 = (bf16[128,2048]{1,0:T(8,128)(2,1)}, bf16[128,2048]{1,0:T(8,128)(2,1)S(1)}, u32[]{:S(2)}, u32[]{:S(2)}) collective-permute-start(bf16[128,2048]{1,0:T(8,128)(2,1)} %get-tuple-element.190.rest_1_.rest_0_), channel_id=1, source_target_pairs={{0,4},{4,0},{1,5},{5,1},{2,6},{6,2},{3,7},{7,3},{8,12},{12,8},{9,1... | collective-permute-start | bytes 1572872 | tf_op jit(solution)/shard_map/ppermute | solution.py:734
  64.8 22.6 %collective-permute-start.8 = (bf16[4,208,192]{2,1,0:T(8,128)(2,1)S(1)}, bf16[4,208,192]{2,1,0:T(8,128)(2,1)S(1)}, u32[]{:S(2)}, u32[]{:S(2)}) collective-permute-start(bf16[4,208,192]{2,1,0:T(8,128)(2,1)S(1)} %pad_maximum_fusion.2.rest_8_), channel_id=1, source_target_pairs={{0,16},{8,24},{16,0},{24,8},{1,17},{9,25},{17,1},{25,9},{2,18},{10... | collective-permute-start | bytes 958472 | tf_op jit(solution)/shard_map/ppermute | solution.py:739
  66.4 52.9 %collective-permute-start.11 = (bf16[4,192,768]{2,1,0:T(8,128)(2,1)}, bf16[4,192,768]{2,1,0:T(8,128)(2,1)S(1)}, u32[]{:S(2)}, u32[]{:S(2)}) collective-permute-start(bf16[4,192,768]{2,1,0:T(8,128)(2,1)} %bitcast.100), channel_id=1, source_target_pairs={{0,16},{8,24},{16,0},{24,8},{1,17},{9,25},{17,1},{25,9},{2,18},{10... | collective-permute-start | bytes 3538952 | tf_op jit(solution)/shard_map/ppermute | solution.py:739
  87.4 39.6 %collective-permute-start.18 = (bf16[4,192,768]{2,1,0:T(8,128)(2,1)}, bf16[4,192,768]{2,1,0:T(8,128)(2,1)}, u32[]{:S(2)}, u32[]{:S(2)}) collective-permute-start(bf16[4,192,768]{2,1,0:T(8,128)(2,1)} %bitcast.102), channel_id=1, source_target_pairs={{0,16},{8,24},{16,0},{24,8},{1,17},{9,25},{17,1},{25,9},{2,18},{10... | collective-permute-start | bytes 3538952 | tf_op jit(solution)/shard_map/ppermute | solution.py:739
  127.8 167.9 %all-gather.18.cloned.1.call-start = ((), (), s32[]{:S(2)}) async-start(), calls=%async_computation.6 | async-start | bytes 3932160 | tf_op jit(solution)/shard_map/all_gather | solution.py:881
  164.5 22.7 %collective-permute-start.21 = (bf16[192,512]{1,0:T(8,128)(2,1)}, bf16[192,512]{1,0:T(8,128)(2,1)S(1)}, u32[]{:S(2)}, u32[]{:S(2)}) collective-permute-start(bf16[192,512]{1,0:T(8,128)(2,1)} %get-tuple-element.243), channel_id=1, source_target_pairs={{0,1},{1,0},{2,3},{3,2},{4,5},{5,4},{6,7},{7,6},{8,9},{9,8},{10,11... | collective-permute-start | bytes 589832 | tf_op jit(solution)/shard_map/ppermute | solution.py:739
  166.2 22.1 %collective-permute-start.22 = (bf16[192,512]{1,0:T(8,128)(2,1)}, bf16[192,512]{1,0:T(8,128)(2,1)S(1)}, u32[]{:S(2)}, u32[]{:S(2)}) collective-permute-start(bf16[192,512]{1,0:T(8,128)(2,1)} %get-tuple-element.244), channel_id=1, source_target_pairs={{0,2},{1,3},{2,0},{3,1},{4,6},{5,7},{6,4},{7,5},{8,10},{9,11},{10,... | collective-permute-start | bytes 589832 | tf_op jit(solution)/shard_map/ppermute | solution.py:739
  167.2 21.1 %collective-permute-start.23 = (bf16[192,512]{1,0:T(8,128)(2,1)}, bf16[192,512]{1,0:T(8,128)(2,1)S(1)}, u32[]{:S(2)}, u32[]{:S(2)}) collective-permute-start(bf16[192,512]{1,0:T(8,128)(2,1)} %get-tuple-element.245), channel_id=1, source_target_pairs={{0,3},{1,2},{2,1},{3,0},{4,7},{5,6},{6,5},{7,4},{8,11},{9,10},{10,... | collective-permute-start | bytes 589832 | tf_op jit(solution)/shard_map/ppermute | solution.py:739
  186.6 17.6 %collective-permute-start.24 = (bf16[4,192,1728]{2,1,0:T(8,128)(2,1)}, bf16[4,192,1728]{2,1,0:T(8,128)(2,1)}, u32[]{:S(2)}, u32[]{:S(2)}) collective-permute-start(bf16[4,192,1728]{2,1,0:T(8,128)(2,1)} %get-tuple-element.254), channel_id=1, source_target_pairs={{0,8},{8,0},{16,24},{24,16},{1,9},{9,1},{17,25},{25,17},{2,10},{10... | collective-permute-start | bytes 7962632 | tf_op jit(solution)/shard_map/ppermute | solution.py:739
  186.7 17.5 %collective-permute-start.25 = (bf16[4,192,1728]{2,1,0:T(8,128)(2,1)}, bf16[4,192,1728]{2,1,0:T(8,128)(2,1)}, u32[]{:S(2)}, u32[]{:S(2)}) collective-permute-start(bf16[4,192,1728]{2,1,0:T(8,128)(2,1)} %get-tuple-element.255), channel_id=1, source_target_pairs={{0,8},{8,0},{16,24},{24,16},{1,9},{9,1},{17,25},{25,17},{2,10},{10... | collective-permute-start | bytes 7962632 | tf_op jit(solution)/shard_map/ppermute | solution.py:739
  211.7 33.6 %collective-permute-start.27 = (bf16[4,96,1728]{2,1,0:T(8,128)(2,1)}, bf16[4,96,1728]{2,1,0:T(8,128)(2,1)}, u32[]{:S(2)}, u32[]{:S(2)}) collective-permute-start(bf16[4,96,1728]{2,1,0:T(8,128)(2,1)} %dynamic-slice_bitcast_fusion), channel_id=1, source_target_pairs={{0,4},{4,0},{1,5},{5,1},{2,6},{6,2},{3,7},{7,3},{8,12},{12,8},{9,1... | collective-permute-start | bytes 3981320 | tf_op jit(solution)/shard_map/ppermute | solution.py:739
  213.2 32.1 %collective-permute-start.26 = (bf16[2,192,1728]{2,1,0:T(8,128)(2,1)}, bf16[2,192,1728]{2,1,0:T(8,128)(2,1)}, u32[]{:S(2)}, u32[]{:S(2)}) collective-permute-start(bf16[2,192,1728]{2,1,0:T(8,128)(2,1)} %get-tuple-element.379), channel_id=1, source_target_pairs={{0,16},{8,24},{16,0},{24,8},{1,17},{9,25},{17,1},{25,9},{2,18},{10... | collective-permute-start | bytes 3981320 | tf_op jit(solution)/shard_map/ppermute | solution.py:739
  213.9 42.5 %collective-permute-start.28 = (bf16[1,128,2048]{2,1,0:T(8,128)(2,1)S(1)}, bf16[1,128,2048]{2,1,0:T(8,128)(2,1)}, u32[]{:S(2)}, u32[]{:S(2)}) collective-permute-start(bf16[1,128,2048]{2,1,0:T(8,128)(2,1)S(1)} %copy-done.36), channel_id=1, source_target_pairs={{0,4},{4,0},{1,5},{5,1},{2,6},{6,2},{3,7},{7,3},{8,12},{12,8},{9,1... | collective-permute-start | bytes 1572872 | tf_op jit(solution)/shard_map/ppermute | solution.py:734
  214.5 176.4 %reduce-scatter.2.cloned.1.call-start = ((), (), s32[]{:S(2)}) async-start(), calls=%async_computation.2 | async-start | bytes 1720320 | tf_op jit(solution)/shard_map/reduce_scatter | solution.py:907
  243.8 35.0 %collective-permute-start.30 = (bf16[2,128,2048]{2,1,0:T(8,128)(2,1)}, bf16[2,128,2048]{2,1,0:T(8,128)(2,1)}, u32[]{:S(2)}, u32[]{:S(2)}) collective-permute-start(bf16[2,128,2048]{2,1,0:T(8,128)(2,1)} %get-tuple-element.269), channel_id=1, source_target_pairs={{0,4},{4,0},{1,5},{5,1},{2,6},{6,2},{3,7},{7,3},{8,12},{12,8},{9,1... | collective-permute-start | bytes 3145736 | tf_op jit(solution)/shard_map/ppermute | solution.py:734
  247.1 47.0 %collective-permute-start.31 = (bf16[2,96,1728]{2,1,0:T(8,128)(2,1)S(1)}, bf16[2,96,1728]{2,1,0:T(8,128)(2,1)S(1)}, u32[]{:S(2)}, u32[]{:S(2)}) collective-permute-start(bf16[2,96,1728]{2,1,0:T(8,128)(2,1)S(1)} %dynamic-slice_bitcast_fusion.1), channel_id=1, source_target_pairs={{0,4},{4,0},{1,5},{5,1},{2,6},{6,2},{3,7},{7,3},{8,12},{12,8},{9,1... | collective-permute-start | bytes 1990664 | tf_op jit(solution)/shard_map/ppermute | solution.py:739
  250.2 25.8 %collective-permute-start.29 = (bf16[2,96,1728]{2,1,0:T(8,128)(2,1)S(1)}, bf16[2,96,1728]{2,1,0:T(8,128)(2,1)S(1)}, u32[]{:S(2)}, u32[]{:S(2)}) collective-permute-start(bf16[2,96,1728]{2,1,0:T(8,128)(2,1)S(1)} %slice.127), channel_id=1, source_target_pairs={{0,16},{8,24},{16,0},{24,8},{1,17},{9,25},{17,1},{25,9},{2,18},{10... | collective-permute-start | bytes 1990664 | tf_op jit(solution)/shard_map/ppermute | solution.py:739
  271.5 24.1 %collective-permute-start.32 = (bf16[192,512]{1,0:T(8,128)(2,1)}, bf16[192,512]{1,0:T(8,128)(2,1)S(1)}, u32[]{:S(2)}, u32[]{:S(2)}) collective-permute-start(bf16[192,512]{1,0:T(8,128)(2,1)} %get-tuple-element.274.rest_1_), channel_id=1, source_target_pairs={{0,1},{1,0},{2,3},{3,2},{4,5},{5,4},{6,7},{7,6},{8,9},{9,8},{10,11... | collective-permute-start | bytes 589832 | tf_op jit(solution)/shard_map/ppermute | solution.py:739
  275.9 19.7 %collective-permute-start.33 = (bf16[192,512]{1,0:T(8,128)(2,1)}, bf16[192,512]{1,0:T(8,128)(2,1)S(1)}, u32[]{:S(2)}, u32[]{:S(2)}) collective-permute-start(bf16[192,512]{1,0:T(8,128)(2,1)} %get-tuple-element.275.rest_2_), channel_id=1, source_target_pairs={{0,2},{1,3},{2,0},{3,1},{4,6},{5,7},{6,4},{7,5},{8,10},{9,11},{10,... | collective-permute-start | bytes 589832 | tf_op jit(solution)/shard_map/ppermute | solution.py:739
  275.9 19.7 %collective-permute-start.34 = (bf16[192,512]{1,0:T(8,128)(2,1)}, bf16[192,512]{1,0:T(8,128)(2,1)S(1)}, u32[]{:S(2)}, u32[]{:S(2)}) collective-permute-start(bf16[192,512]{1,0:T(8,128)(2,1)} %get-tuple-element.276.rest_3_), channel_id=1, source_target_pairs={{0,3},{1,2},{2,1},{3,0},{4,7},{5,6},{6,5},{7,4},{8,11},{9,10},{10,... | collective-permute-start | bytes 589832 | tf_op jit(solution)/shard_map/ppermute | solution.py:739
  295.7 135.7 %all-gather.10.cloned.1.call-start = ((), (), s32[]{:S(2)}) async-start(), calls=%async_computation.1 | async-start | bytes 3932160 | tf_op jit(solution)/shard_map/all_gather | solution.py:923
  296.1 21.9 %collective-permute-start.35 = (bf16[192,512]{1,0:T(8,128)(2,1)S(1)}, bf16[192,512]{1,0:T(8,128)(2,1)S(1)}, u32[]{:S(2)}, u32[]{:S(2)}) collective-permute-start(bf16[192,512]{1,0:T(8,128)(2,1)S(1)} %copy-done.44), channel_id=1, source_target_pairs={{0,1},{1,0},{2,3},{3,2},{4,5},{5,4},{6,7},{7,6},{8,9},{9,8},{10,11... | collective-permute-start | bytes 589832 | tf_op jit(solution)/shard_map/ppermute | solution.py:739
  300.4 25.4 %collective-permute-start.36 = (bf16[192,512]{1,0:T(8,128)(2,1)S(1)}, bf16[192,512]{1,0:T(8,128)(2,1)S(1)}, u32[]{:S(2)}, u32[]{:S(2)}) collective-permute-start(bf16[192,512]{1,0:T(8,128)(2,1)S(1)} %copy-done.45), channel_id=1, source_target_pairs={{0,2},{1,3},{2,0},{3,1},{4,6},{5,7},{6,4},{7,5},{8,10},{9,11},{10,... | collective-permute-start | bytes 589832 | tf_op jit(solution)/shard_map/ppermute | solution.py:739
  300.4 25.4 %collective-permute-start.37 = (bf16[192,512]{1,0:T(8,128)(2,1)S(1)}, bf16[192,512]{1,0:T(8,128)(2,1)S(1)}, u32[]{:S(2)}, u32[]{:S(2)}) collective-permute-start(bf16[192,512]{1,0:T(8,128)(2,1)S(1)} %copy-done.46), channel_id=1, source_target_pairs={{0,3},{1,2},{2,1},{3,0},{4,7},{5,6},{6,5},{7,4},{8,11},{9,10},{10,... | collective-permute-start | bytes 589832 | tf_op jit(solution)/shard_map/ppermute | solution.py:739
  325.8 24.3 %collective-permute-start.38 = (bf16[192,512]{1,0:T(8,128)(2,1)}, bf16[192,512]{1,0:T(8,128)(2,1)S(1)}, u32[]{:S(2)}, u32[]{:S(2)}) collective-permute-start(bf16[192,512]{1,0:T(8,128)(2,1)} %get-tuple-element.294.rest_9_), channel_id=1, source_target_pairs={{0,1},{1,0},{2,3},{3,2},{4,5},{5,4},{6,7},{7,6},{8,9},{9,8},{10,11... | collective-permute-start | bytes 589832 | tf_op jit(solution)/shard_map/ppermute | solution.py:739
  337.3 15.5 %collective-permute-start.40 = (bf16[192,512]{1,0:T(8,128)(2,1)}, bf16[192,512]{1,0:T(8,128)(2,1)S(1)}, u32[]{:S(2)}, u32[]{:S(2)}) collective-permute-start(bf16[192,512]{1,0:T(8,128)(2,1)} %get-tuple-element.296.rest_11_), channel_id=1, source_target_pairs={{0,3},{1,2},{2,1},{3,0},{4,7},{5,6},{6,5},{7,4},{8,11},{9,10},{10,... | collective-permute-start | bytes 589832 | tf_op jit(solution)/shard_map/ppermute | solution.py:739
  352.9 15.7 %collective-permute-start.41 = (f32[100,256]{1,0:T(8,128)S(1)}, f32[100,256]{1,0:T(8,128)S(1)}, u32[]{:S(2)}, u32[]{:S(2)}) collective-permute-start(f32[100,256]{1,0:T(8,128)S(1)} %concatenate.31), channel_id=1, source_target_pairs={{0,1},{1,0},{2,3},{3,2},{4,5},{5,4},{6,7},{7,6},{8,9},{9,8},{10,11... | collective-permute-start | bytes 307208 | tf_op jit(solution)/shard_map/ppermute | solution.py:739
  (72 other events, 726.6 us)
Sparse Core Ops, SparseCore 0:
  9.6 42.4 all-gather.11
  53.6 28.9 all-gather.13
  127.9 54.9 all-gather.15
  214.6 65.5 all-gather.17
  295.8 44.5 reduce-scatter.1
  368.7 62.6 all-gather.9

commit v2 on v1

--- a/solution.py
+++ b/solution.py
@@ -330,7 +330,9 @@
         out_shape=shapes + [jax.ShapeDtypeStruct((64, 256), f32)],
         compiler_params=pltpu.CompilerParams(vmem_limit_bytes=VMEM),
         cost_estimate=pl.CostEstimate(
-            flops=(2 if dt is not None else 40) * n * T * KB * 1280, bytes_accessed=n * T * 3000, transcendentals=n * T * KB
+            flops=(2 if dt is not None else 40) * n * T * KB * 1280,
+            bytes_accessed=n * T * 3000,
+            transcendentals=n * T * KB,
         ),
         name="attn_bwd",
     )(sc, *args)
@@ -442,12 +444,24 @@
     )
 
 
-def mlpa_kernel(sc_ref, x_ref, v_ref, *rest, nt, fb):
+def piece_specs(w):
+    _, dd, cols = w[0].shape
+    return [pl.BlockSpec((None, dd, cols), lambda k, s: (s[1] ^ k, 0, 0))] * 4
+
+
+def assemble(sc_ref, whole, parts):
+    for r, p in enumerate(parts):
+        whole[rows_of(sc_ref, r, p.shape[0]), :] = p[...]
+
+
+def mlp1_kernel(sc_ref, x_ref, g_ref, v_ref, *rest, nt, fb):
     no = 2 * nt
-    os, ps, p1, rest = rest[:no], rest[no : no + 4], rest[no + 4 : no + 8], rest[no + 8 :]
-    a_ref, sl_ref, h2_ref, y1_ref, wt_ref, wp, b4, bias, wi = rest
-    dd, ft = p1[0].shape
-    D = 4 * dd
+    os, ps, rest = rest[:no], rest[no : no + 4], rest[no + 4 :]
+    p1, p2, rest = rest[:4], rest[4:8], rest[8:]
+    a_ref, du_ref, h2_ref, da_ref, y1_ref, dy_ref, sm_ref, db_ref, *rest = rest
+    dos, (dh, wp, wts, b4, bias, wi, wo) = rest[:nt], rest[nt:]
+    D, ft = wi.shape
+    dd = D // 4
     k = pl.program_id(0)
 
     @pl.when(k == 0)
@@ -458,14 +472,16 @@
             for r in range(4):
                 wp[rows_of(sc_ref, r, dd), :] = ps[r][kk, 0:dd]
             wt = wp[...].T
-            wt_ref[kk] = wt
+            wts[kk] = wt
             y = y + dot(os[kk][...], wt[:na], 0, 0)
             y = y + dot(os[nt + kk][...], wt[na:], 0, 0)
         y1_ref[...] = y
         xh, _ = norm_parts(y)
         h2_ref[...] = (xh * v_ref[2:3, :] + v_ref[3:4, :]).astype(bf16)
+        dh[...] = jnp.zeros_like(dh)
 
     assemble(sc_ref, wi, p1)
+    assemble(sc_ref, wo, p2)
     for r in range(4):
         b4[sc_ref[2] ^ r] = ps[r][k, dd:, :].astype(f32)
     rows = jnp.concatenate([b4[j, :, 0:16] for j in range(4)], 1)
@@ -474,67 +490,11 @@
     for j in range(ft // fb):
         sl = slice(j * fb, (j + 1) * fb)
         u = jnp.dot(h2_ref[...], wi[:, sl], preferred_element_type=f32) + bias[:, sl]
+        ga = jnp.dot(g_ref[...], wo[:, sl], preferred_element_type=f32)
         cdf = 0.5 + 0.5 * lax.erf(u * 0.7071067811865476)
         a_ref[:, sl] = (u * cdf).astype(bf16)
         slope = cdf + u * (jnp.exp(-0.5 * u * u) * 0.3989422804014327)
-        sl_ref[:, sl] = slope.astype(sl_ref.dtype)
-
-
-def piece_specs(w):
-    n2, dd, cols = w[0].shape
-    at = lambda add: pl.BlockSpec((None, dd, cols), lambda k, s: (add + (s[1] ^ k), 0, 0))
-    return [at(0), at(0), at(n2 // 2), at(n2 // 2)]
-
-
-def pieces(w):
-    return [w[0], w[1], w[0], w[1]]
-
-
-def assemble(sc_ref, whole, parts):
-    for r, p in enumerate(parts):
-        whole[rows_of(sc_ref, r, p.shape[0]), :] = p[...]
-
-
-def mlpa(sc, x, vecs, os, ps, p1):
-    D = x.shape[1]
-    nt, ft = ps[0].shape[0], p1[0].shape[2]
-    N = os[0].shape[1]
-    kt = ps[0].shape[2]
-    mine = pl.BlockSpec((N, D), lambda k, s: (s[1], 0))
-    act = pl.BlockSpec((None, N, ft), lambda k, s: (k, 0, 0))
-    full = whole_spec((N, D))
-    return call(
-        functools.partial(mlpa_kernel, nt=nt, fb=256), sc, (nt,),
-        [mine, whole_spec(vecs.shape)]
-        + [whole_spec(o.shape) for o in os]
-        + [whole_spec(p.shape) for p in ps]
-        + piece_specs(p1),
-        [x, vecs, *os, *ps, *pieces(p1)],
-        [act, act, full, full, whole_spec((nt, kt, D))],
-        [((nt, N, ft), bf16), ((nt, N, ft), f32), ((N, D), bf16), ((N, D), f32)]
-        + [((nt, kt, D), bf16)],
-        [pltpu.VMEM((D, kt), bf16), pltpu.VMEM((4, 16, kt), f32), pltpu.VMEM((1, ft), f32)]
-        + [pltpu.VMEM((D, ft), bf16)],
-        "mlp_in", 3 * N * D * ft * nt, 24 * 2**20,
-    )
-
-
-def mlpb_kernel(sc_ref, g_ref, v_ref, y1_ref, sl_ref, *rest, nt, fb):
-    wt_ref, p1, p2, rest = rest[0], rest[1:5], rest[5:9], rest[9:]
-    du_ref, da_ref, dy_ref, sm_ref, db_ref, *dos, dh, wi, wo = rest
-    D, ft = wi.shape
-    k = pl.program_id(0)
-
-    @pl.when(k == 0)
-    def _():
-        dh[...] = jnp.zeros_like(dh)
-
-    assemble(sc_ref, wo, p2)
-    assemble(sc_ref, wi, p1)
-    for j in range(ft // fb):
-        sl = slice(j * fb, (j + 1) * fb)
-        ga = jnp.dot(g_ref[...], wo[:, sl], preferred_element_type=f32)
-        du = (sl_ref[:, sl] * ga).astype(bf16)
+        du = (slope * ga).astype(bf16)
         du_ref[:, sl] = du
         db_ref[:, sl] = jnp.sum(du.astype(f32), axis=0, keepdims=True)
         dh[...] += dot(du, wi[:, sl], 1, 1)
@@ -548,31 +508,45 @@
         dy_ref[...] = dy
         da = dy.astype(bf16)
         da_ref[...] = da
+        for kk in range(nt):
+            dos[kk][...] = dot(wts[kk], da, 1, 1).astype(bf16)
         sums = [jnp.sum(z, axis=0, keepdims=True) for z in (d * xh, d, da.astype(f32), g)]
         sm_ref[...] = jnp.concatenate(sums + [jnp.zeros((4, D), f32)], 0)
-        for kk in range(nt):
-            dos[kk][...] = dot(wt_ref[kk], da, 1, 1).astype(bf16)
-
-
-def mlpb(sc, g, vecs, y1, slope, wt, p1, p2):
-    N, D = y1.shape
-    nt, kt = wt.shape[:2]
+
+
+def mlp1(sc, x, g, vecs, os, ps, p1, p2):
+    D = x.shape[1]
+    nt, _, kt = ps[0].shape
     ft = p1[0].shape[2]
+    N = os[0].shape[1]
+    mine = pl.BlockSpec((N, D), lambda k, s: (s[1], 0))
     act = pl.BlockSpec((None, N, ft), lambda k, s: (k, 0, 0))
     row = pl.BlockSpec((None, 1, ft), lambda k, s: (s[1] ^ k, 0, 0))
     full = whole_spec((N, D))
     return call(
-        functools.partial(mlpb_kernel, nt=nt, fb=256), sc, (nt,),
-        [pl.BlockSpec((N, D), lambda k, s: (s[1], 0)), whole_spec(vecs.shape), full, act]
-        + [whole_spec(wt.shape)]
+        functools.partial(mlp1_kernel, nt=nt, fb=256), sc, (nt,),
+        [mine, mine, whole_spec(vecs.shape)]
+        + [whole_spec(o.shape) for o in os]
+        + [whole_spec(p.shape) for p in ps]
         + piece_specs(p1)
         + piece_specs(p2),
-        [g, vecs, y1, slope, wt, *pieces(p1), *pieces(p2)],
-        [act, full, full, whole_spec((8, D)), row] + [whole_spec((kt, N))] * nt,
-        [((nt, N, ft), bf16), ((N, D), bf16), ((N, D), f32), ((8, D), f32), ((nt, 1, ft), f32)]
+        [x, g, vecs, *os, *ps, *p1, *p2],
+        [act, act, full, full, full, full, whole_spec((8, D)), row] + [whole_spec((kt, N))] * nt,
+        [((nt, N, ft), bf16)] * 2
+        + [((N, D), bf16)] * 2
+        + [((N, D), f32)] * 2
+        + [((8, D), f32), ((nt, 1, ft), f32)]
         + [((kt, N), bf16)] * nt,
-        [pltpu.VMEM((N, D), f32)] + [pltpu.VMEM((D, ft), bf16)] * 2,
-        "mlp_grad", 5 * N * D * ft * nt, 24 * 2**20,
+        [
+            pltpu.VMEM((N, D), f32),
+            pltpu.VMEM((D, kt), bf16),
+            pltpu.VMEM((nt, kt, D), bf16),
+            pltpu.VMEM((4, 16, kt), f32),
+            pltpu.VMEM((1, ft), f32),
+            pltpu.VMEM((D, ft), bf16),
+            pltpu.VMEM((D, ft), bf16),
+        ],
+        "mlp_grad", 6 * N * D * ft * nt, 24 * 2**20,
     )
 
 
@@ -630,7 +604,7 @@
         + [act, act]
         + [whole_spec(o.shape) for o in os]
         + piece_specs(p2),
-        [g, vecs, h2, da, y1, a, du, *os, *pieces(p2)],
+        [g, vecs, h2, da, y1, a, du, *os, *p2],
         [gw] * 4 + [full],
         [((nt, dd, cols), bf16)] * 4 + [((N, D), bf16)],
         [pltpu.VMEM((D, N), bf16)] * 3
@@ -687,7 +661,8 @@
 
 
 def dh1_kernel(sc_ref, x_ref, dy_ref, v_ref, *rest, nt, H):
-    dx, (p3, gi_ref, da) = rest[: H * nt], rest[H * nt :]
+    dx, (p3, p3b, gi_ref, da, w3) = rest[: H * nt], rest[H * nt :]
+    hd = p3.shape[2]
     D = x_ref.shape[1]
     E3 = H * 192
     for k in range(nt):
@@ -695,13 +670,15 @@
             da[(k * H + h) * 192 : (k * H + h + 1) * 192, :] = dx[h * nt + k][...]
     t = jnp.zeros((D, da.shape[1]), f32)
     for k in range(nt):
-        w = p3[:, sc_ref[1] ^ k].reshape(D, E3)
-        t = t + jnp.dot(w, da[k * E3 : (k + 1) * E3, :], preferred_element_type=f32)
+        for j in range(4):
+            w3[2 * j * hd : (2 * j + 1) * hd, :] = p3[j, sc_ref[1] ^ k]
+            w3[(2 * j + 1) * hd : (2 * j + 2) * hd, :] = p3b[j, sc_ref[1] ^ k]
+        t = t + jnp.dot(w3[...], da[k * E3 : (k + 1) * E3, :], preferred_element_type=f32)
     xh, r = norm_parts(x_ref[...].astype(f32))
     gi_ref[...] = (dy_ref[...] + norm_back(t.T, v_ref[0:1, :], xh, r)).astype(bf16)
 
 
-def dh1(sc, x, dy1, vecs, dx, p3):
+def dh1(sc, x, dy1, vecs, dx, p3, p3b):
     N, D = dy1.shape
     nt = p3.shape[1]
     H = len(dx) // nt
@@ -709,11 +686,11 @@
         functools.partial(dh1_kernel, nt=nt, H=H), sc, (1,),
         [pl.BlockSpec((N, D), lambda k, s: (s[1], 0)), whole_spec((N, D)), whole_spec(vecs.shape)]
         + [whole_spec((192, N))] * len(dx)
-        + [whole_spec(p3.shape)],
-        [x, dy1, vecs, *dx, p3],
+        + [whole_spec(p3.shape)] * 2,
+        [x, dy1, vecs, *dx, p3, p3b],
         [whole_spec((N, D))],
         [((N, D), bf16)],
-        [pltpu.VMEM((nt * H * 192, N), bf16)],
+        [pltpu.VMEM((nt * H * 192, N), bf16), pltpu.VMEM((D, H * 192), bf16)],
         "norm1_grad", 2 * N * D * D * 3, 8 * 2**20,
     )[0]
 
@@ -831,26 +808,26 @@
             scalars(nc - 1), h0, qT, kv_far[-1][h0:h1], tab, state, True, R, nt
         )
         if h0 == 0:
-            state, far, p2 = bar((state, far, p2))
+            state, far, p2, o0, o1, o2, o3, kv_far[-1][-1] = bar(
+                (state, far, p2, o0, o1, o2, o3, kv_far[-1][-1])
+            )
             p2x = flip(p2, "dp", 2)
             ps = [own, flip(own, "dp", 1), far, flip(far, "dp", 1)]
         else:
             o0, ps, p1, p1x, os = bar((o0, ps, p1, p1x, os))
-            p1 = jnp.concatenate([p1, p1x])
-            p1 = (p1, flip(p1, "dp", 1))
+            p1 = (p1, flip(p1, "dp", 1), p1x, flip(p1x, "dp", 1))
         os += spread([o0, o1, o2, o3])
     o32, lse = state
     os, p2x = bar((os, p2x))
-    p2 = jnp.concatenate([p2, p2x])
-    p2 = (p2, flip(p2, "dp", 1))
-    p3 = gather_weights(after(small[0], *os)[:dd])
-    a, slope, h2, y1, wt = mlpa(sc, x2, vecs, os, ps, p1)
-    du, da, dy1, sm2, dbin, *dos = mlpb(sc, g2, vecs, y1, slope, wt, p1, p2)
+    p2 = (p2, flip(p2, "dp", 1), p2x, flip(p2x, "dp", 1))
+    w0 = after(small[0], *os)[:dd]
+    p3a = gather_weights(w0[: dd // 2])
+    a, du, h2, da, y1, dy1, sm2, dbin, *dos = mlp1(sc, x2, g2, vecs, os, ps, p1, p2)
     dos = spread(dos)
     *gws, out = mlp2(sc, g2, vecs, h2, da, y1, a, du, os, p2)
 
     add = lambda *v: sum(z.astype(f32) for z in v).astype(bf16)
-    out, dos, p3 = bar((out, dos, p3))
+    out, dos, p3a = bar((out, dos, p3a))
     core = [flip(gws[1], "dp", 1), flip(gws[3], "dp", 1)]
     halves = nc == 2
     part = lambda v, i: lax.dynamic_index_in_dim(
@@ -896,6 +873,8 @@
         dx += d
         if h == 0 and halves:
             dtab, xb = bar((dtab, xb))
+        if h == 0:
+            p3b = gather_weights(after(w0, block_out, dtab)[dd // 2 :])
         if h == 1:
             if halves:
                 dtab, ya = bar((dtab, ya))
@@ -904,6 +883,7 @@
         if h == 2:
             dtab, dxr, xh1 = bar((dtab, dxr, xh1))
         dxr = dxr + spread(d)
+    v = after(v, dtab)
     gsum = lax.psum_scatter(v, "tensor", scatter_dimension=0)
 
     keepq, sendq, bq, sm1 = gqkv(sc, xh1, vecs, wT, dx, nt)
@@ -915,10 +895,10 @@
     flat = jnp.concatenate(
         [z.reshape(-1, 256) for z in (sm2[:4], sm1[:2], dbin, bq)] + [dtab]
     )
-    flat, sendq, dxr = bar((flat, sendq, dxr))
+    flat, sendq, dxr[-3] = bar((flat, sendq, dxr[-3]))
     flats = [flat] + [flip(flat, "tensor", k) for k in range(1, nt)]
 
-    gin = dh1(sc, x2, dy1, vecs, dxr, p3)
+    gin = dh1(sc, x2, dy1, vecs, dxr, p3a, p3b)
     gin, sendq, flats = bar((gin, sendq, flats))
     gall = lax.all_gather(gin, "tensor", axis=0, tiled=True)
     while len(flats) > 1:

time: 455 us -> 454 us (level)
  waiting for transfers between devices: 89.8 us -> 108 us
  starting transfers between devices: 77.1 us -> 64.3 us
  Pallas kernels: 224 us -> 216 us
    ppermute x46 -> x48, waiting for transfers between devices: 46.8 us -> 76.8 us  [flip(): return lax.ppermute(value, axis, [(s, s ^ bit) for s in range(n)])]
    ppermute x5, waiting for transfers between devices: 15.1 us -> 0.01 us  [shift(): return lax.ppermute(value, axis, [(s, (s + steps) % n) for s in range(n)])]
    ppermute x46 -> x48, starting transfers between devices: 71 us -> 59 us  [flip(): return lax.ppermute(value, axis, [(s, s ^ bit) for s in range(n)])]
    pallas_call x8 -> x7, Pallas kernels: 81 us -> 73.2 us  [call(): pl.pallas_call(kernel, grid_spec=pltpu.PrefetchScalarGridSpec(num_scalar_...]
    unnamed x102 -> x78, local copies, waits for them, and re-layouts: 11.1 us -> 11.5 us
  transfers between devices with their start and end apart: 57 -> 60, of which waited for: 20 -> 22; matrix products, arithmetic and copies ran while one was open for 4% -> 6% of each run, Pallas kernels for 50% -> 49%
where the time goes in v2:
time: 454 us; the launch traced here: 445 us
  Pallas kernels  216 us (48%)
  waiting for transfers between devices  108 us (24%)
  starting transfers between devices  64.3 us (14%)
  local copies, waits for them, and re-layouts  22.2 us (5%)
  other arithmetic  19.1 us (4%)
  between operations  15.1 us (3%)
    pallas_call x5, Pallas kernels, attn_bwd(): pl.pallas_call(functools.partial(bwd_kernel, R=R, bk=bk, has_dq=dq is not...  89.8 us
    ppermute x48, waiting for transfers between devices, flip(): return lax.ppermute(value, axis, [(s, s ^ bit) for s in range(n)])  76.8 us
    pallas_call x7, Pallas kernels, call(): pl.pallas_call(kernel, grid_spec=pltpu.PrefetchScalarGridSpec(num_scalar_...  73.2 us
    ppermute x48, starting transfers between devices, flip(): return lax.ppermute(value, axis, [(s, s ^ bit) for s in range(n)])  59 us
    pallas_call x3, Pallas kernels, attn_fwd(): pl.pallas_call(functools.partial(fwd_kernel, R=R, bk=bk, first=first, las...  53.3 us
    all_gather x1, waiting for transfers between devices, per_device(): gall = lax.all_gather(gin, 'tensor', axis=0, tiled=True)  28.7 us
    unnamed x78, local copies, waits for them, and re-layouts  11.5 us
  transfers between devices with their start and end apart: 60, of which 22 were waited for; matrix products, arithmetic and copies ran while one was open for 6% of the time, Pallas kernels for 49%

profile of v2, /device:TPU:0, one launch (start us, length us, event | category | flops | bytes accessed | tf_op | source)
XLA Modules:
  0.0 444.8 jit_solution(14804579240928710783)
XLA Ops:
  8.6 2.6 pack.1.s0
  18.5 2.7 collective-permute-done
  22.0 5.8 %collective-permute-done.3.s3 = bf16[224,576]{1,0:T(8,128)(2,1)S(1)} collective-permute-done((bf16[224,576]{1,0:T(8,128)(2,1)}, bf16[224,576]{1,0:T(8,128)(2,1)S(1)}, u32[]{:S(2)}, u32[]{:S(2)}) %collective-permute-start.3) | collective-permute-done | bytes 258080 | tf_op jit(solution)/shard_map/ppermute | solution.py:716
  27.8 2.7 collective-permute-start.6
  30.5 8.8 %front.1 = (bf16[64,384]{1,0:T(8,128)(2,1)}, f32[8,768]{1,0:T(8,128)}, bf16[3,64,2048]{2,1,0:T(8,128)(2,1)}, bf16[128,2048]{1,0:T(8,128)(2,1)}, bf16[128,2048]{1...) custom-call(s32[3]{0:T(128)} %add_add_fusion.1.sc_ref, ...), custom_call_target="tpu_custom_call" | custom-call | flops 1811939328 | bytes 9437184 | tf_op jit(solution)/shard_map/front/pallas_call | solution.py:363
  42.9 23.3 %attn_fwd.3 = (f32[3,64,2048]{2,1,0:T(8,128)}, f32[3,8,2048]{2,1,0:T(8,128)}) custom-call(s32[3]{0:T(128)} %add_add_fusion.1.sc_ref, bf16[3,64,2048]{2,1,0:T(8,128)(2,1)} %get-tuple-element.180.qT_ref, bf16[64,384]{1,0:T(8,128)(2,1)} %get-tuple-element.181.tab_ref, bf16[128,2048]{1,0:T(8,128)(2,1)} %get-tuple-element.182.rest_0_, ...), custom_call_target="tpu_custom_call" | custom-call | flops 12884901888 | bytes 7372800 | tf_op jit(solution)/shard_map/attn_fwd/pallas_call | solution.py:152
  70.0 19.8 %attn_fwd.4 = (f32[3,64,2048]{2,1,0:T(8,128)}, f32[3,8,2048]{2,1,0:T(8,128)}, bf16[128,512]{1,0:T(8,128)(2,1)}, bf16[128,512]{1,0:T(8,128)(2,1)}, bf16[128,512]{1,0:T(8,128)(2,1)}, /*index=5*/bf16[128,512]{1,0:T(8,128)(2,1)}) custom-call(s32[3]{0:T(128)} %add_add_fusion.2.sc_ref, ...), custom_call_target="tpu_custom_call", output_to_operand_aliasing={{0}: (5, {}), {1}: (6, {})} | custom-call | flops 8589934592 | bytes 4915200 | tf_op jit(solution)/shard_map/attn_fwd/pallas_call | solution.py:152
  95.3 2.9 collective-permute-done.12.rest_1_
  99.9 10.2 %attn_fwd.5 = (f32[3,64,2048]{2,1,0:T(8,128)}, f32[3,8,2048]{2,1,0:T(8,128)}, bf16[64,512]{1,0:T(8,128)(2,1)}, bf16[64,512]{1,0:T(8,128)(2,1)}, bf16[64,512]{1,0:T(8,128)(2,1)}, /*index=5*/bf16[64,512]{1,0:T(8,128)(2,1)}) custom-call(s32[3]{0:T(128)} %add_add_fusion.2.sc_ref, ...), custom_call_target="tpu_custom_call", output_to_operand_aliasing={{0}: (4, {}), {1}: (5, {})} | custom-call | flops 4294967296 | bytes 2457600 | tf_op jit(solution)/shard_map/attn_fwd/pallas_call | solution.py:152
  117.3 2.7 collective-permute-done.17.rest_7_
  120.0 8.2 %collective-permute-done.18.rest_18_.rest_10_ = bf16[4,192,768]{2,1,0:T(8,128)(2,1)} collective-permute-done((bf16[4,192,768]{2,1,0:T(8,128)(2,1)}, bf16[4,192,768]{2,1,0:T(8,128)(2,1)}, u32[]{:S(2)}, u32[]{:S(2)}) %collective-permute-start.18) | collective-permute-done | bytes 1179680 | tf_op jit(solution)/shard_map/ppermute | solution.py:716
  132.0 3.4 collective-permute-done.19.rest_13_
  137.3 23.3 %mlp_grad.1 = (bf16[4,512,768]{2,1,0:T(8,128)(2,1)}, bf16[4,512,768]{2,1,0:T(8,128)(2,1)}, bf16[512,768]{1,0:T(8,128)(2,1)}, bf16[512,768]{1,0:T(8,128)(2,1)}, f...) custom-call(s32[3]{0:T(128)} %add_add_fusion.1.sc_ref, ...), custom_call_target="tpu_custom_call" | custom-call | flops 7247757312 | bytes 25165824 | tf_op jit(solution)/shard_map/mlp_grad/pallas_call | solution.py:363
  165.1 17.4 %mlp_weights.1 = (bf16[4,192,1728]{2,1,0:T(8,128)(2,1)}, bf16[4,192,1728]{2,1,0:T(8,128)(2,1)}, bf16[4,192,1728]{2,1,0:T(8,128)(2,1)}, bf16[4,192,1728]{2,1,0:T(8,128)(2,1)}, bf16[512,768]{1,0:T(8,128)(2,1)}) custom-call(s32[3]{0:T(128)} %add_add_fusion.1.sc_ref, bf16[2048,768]{1,0:T(8,128)(2,1)} %bitcast.121, f32[8,768]{1,0:T(8,128)} %get-tuple-element.179.v_ref, ...), custom_call_target="tpu_custom_call" | custom-call | flops 8455716864 | bytes 25165824 | tf_op jit(solution)/shard_map/mlp_weights/pallas_call | solution.py:363
  183.9 14.7 %attn_bwd.5 = (f32[1,64,2048]{2,1,0:T(8,128)}, bf16[1,128,2048]{2,1,0:T(8,128)(2,1)}, f32[64,256]{1,0:T(8,128)}) custom-call(s32[3]{0:T(128)} %add_add_fusion.2.sc_ref, bf16[3,64,2048]{2,1,0:T(8,128)(2,1)} %get-tuple-element.180.qT_ref, bf16[64,384]{1,0:T(8,128)(2,1)} %get-tuple-element.181.tab_ref, bf16[128,2048]{1,0:T(8,128)(2,1)} %copy-done.19, ...), custom_call_target="tpu_custom_call" | custom-call | flops 214748364800 | bytes 6144000 | tf_op jit(solution)/shard_map/attn_bwd/pallas_call | solution.py:318
  199.1 5.5 %add_convert_fusion = (bf16[4,192,1728]{2,1,0:T(8,128)(2,1)S(1)}, bf16[4,192,1728]{2,1,0:T(8,128)(2,1)S(1)}) fusion(bf16[4,192,1728]{2,1,0:T(8,128)(2,1)} %collective-permute-done.26, bf16[4,192,1728]{2,1,0:T(8,128)(2,1)} %get-tuple-element.258, bf16[4,192,1728]{2,1,0:T(8,128)(2,1)} %collective-permute-done.27, bf16[4,192,1728]{2,1,0:T(8,128)(2,1)} %get-tuple-element.256), kind=kLoop, calls=%fused_computation | loop fusion | flops 10616832 | bytes 15925248 | tf_op jit(solution)/shard_map/convert_element_type | solution.py:829
  209.4 29.2 %attn_bwd.6 = (f32[2,64,2048]{2,1,0:T(8,128)}, bf16[2,128,2048]{2,1,0:T(8,128)(2,1)}, f32[64,256]{1,0:T(8,128)}) custom-call(s32[3]{0:T(128)} %add_add_fusion.2.sc_ref, bf16[3,64,2048]{2,1,0:T(8,128)(2,1)} %get-tuple-element.180.qT_ref, bf16[64,384]{1,0:T(8,128)(2,1)} %get-tuple-element.181.tab_ref, bf16[128,2048]{1,0:T(8,128)(2,1)} %copy-done.17, ...), custom_call_target="tpu_custom_call" | custom-call | flops 21474836480 | bytes 12288000 | tf_op jit(solution)/shard_map/attn_bwd/pallas_call | solution.py:318
  239.1 4.0 collective-permute-done.29
  247.5 15.3 %attn_bwd.7 = (bf16[192,512]{1,0:T(8,128)(2,1)}, bf16[192,512]{1,0:T(8,128)(2,1)}, bf16[192,512]{1,0:T(8,128)(2,1)}, bf16[192,512]{1,0:T(8,128)(2,1)}, f32[64,256]{1,0:T(8,128)}) custom-call(s32[3]{0:T(128)} %add_add_fusion.1.sc_ref, bf16[3,64,2048]{2,1,0:T(8,128)(2,1)} %get-tuple-element.180.qT_ref, bf16[64,384]{1,0:T(8,128)(2,1)} %get-tuple-element.181.tab_ref, ...), custom_call_target="tpu_custom_call" | custom-call | flops 10737418240 | bytes 6144000 | tf_op jit(solution)/shard_map/attn_bwd/pallas_call | solution.py:318
  270.2 15.2 %attn_bwd.8 = (bf16[192,512]{1,0:T(8,128)(2,1)}, bf16[192,512]{1,0:T(8,128)(2,1)}, bf16[192,512]{1,0:T(8,128)(2,1)}, bf16[192,512]{1,0:T(8,128)(2,1)}, f32[64,256]{1,0:T(8,128)}) custom-call(s32[3]{0:T(128)} %add_add_fusion.1.sc_ref, bf16[3,64,2048]{2,1,0:T(8,128)(2,1)} %get-tuple-element.180.qT_ref, bf16[64,384]{1,0:T(8,128)(2,1)} %get-tuple-element.181.tab_ref, ...), custom_call_target="tpu_custom_call" | custom-call | flops 10737418240 | bytes 6144000 | tf_op jit(solution)/shard_map/attn_bwd/pallas_call | solution.py:318
  293.0 15.5 %attn_bwd.9 = (bf16[192,512]{1,0:T(8,128)(2,1)}, bf16[192,512]{1,0:T(8,128)(2,1)}, bf16[192,512]{1,0:T(8,128)(2,1)}, bf16[192,512]{1,0:T(8,128)(2,1)}, f32[64,256]{1,0:T(8,128)}) custom-call(s32[3]{0:T(128)} %add_add_fusion.1.sc_ref, bf16[3,64,2048]{2,1,0:T(8,128)(2,1)} %get-tuple-element.180.qT_ref, bf16[64,384]{1,0:T(8,128)(2,1)} %get-tuple-element.181.tab_ref, ...), custom_call_target="tpu_custom_call" | custom-call | flops 10737418240 | bytes 6144000 | tf_op jit(solution)/shard_map/attn_bwd/pallas_call | solution.py:318
  310.2 5.5 %collective-permute-start.40 = (bf16[192,512]{1,0:T(8,128)(2,1)}, bf16[192,512]{1,0:T(8,128)(2,1)S(1)}, u32[]{:S(2)}, u32[]{:S(2)}) collective-permute-start(bf16[192,512]{1,0:T(8,128)(2,1)} %get-tuple-element.299.rest_9_), channel_id=1, source_target_pairs={{0,1},{1,0},{2,3},{3,2},{4,5},{5,4},{6,7},{7,6},{8,9},{9,8},{10,11... | collective-permute-start | bytes 589832 | tf_op jit(solution)/shard_map/ppermute | solution.py:716
  318.1 7.3 %qkv_weights.1 = (bf16[2,192,576]{2,1,0:T(8,128)(2,1)}, bf16[2,192,576]{2,1,0:T(8,128)(2,1)}, f32[3,192,128]{2,1,0:T(8,128)}, f32[8,768]{1,0:T(8,128)}) custom-call(s32[3]{0:T(128)} %add_add_fusion.1.sc_ref, bf16[4,512,768]{2,1,0:T(8,128)(2,1)} %bitcast.129, f32[8,768]{1,0:T(8,128)} %get-tuple-element.179.v_ref, bf16[576,768]{1,0:T(8,128)(2,1)} %get-tuple-element.298.wt_ref, ...), custom_call_target="tpu_custom_call" | custom-call | flops 1811939328 | bytes 8388608 | tf_op jit(solution)/shard_map/qkv_weights/pallas_call | solution.py:363
  332.6 7.4 %collective-permute-done.41.rest_10_ = bf16[192,512]{1,0:T(8,128)(2,1)S(1)} collective-permute-done((bf16[192,512]{1,0:T(8,128)(2,1)}, bf16[192,512]{1,0:T(8,128)(2,1)S(1)}, u32[]{:S(2)}, u32[]{:S(2)}) %collective-permute-start.41) | collective-permute-done | bytes 196640 | tf_op jit(solution)/shard_map/ppermute | solution.py:716
  340.7 8.8 %norm1_grad.1 = bf16[512,768]{1,0:T(8,128)(2,1)} custom-call(s32[3]{0:T(128)} %add_add_fusion.1.sc_ref, bf16[2048,768]{1,0:T(8,128)(2,1)} %bitcast.95, f32[512,768]{1,0:T(8,128)} %get-tuple-element.231.dy_ref, f32[8,768]{1,0:T(8,128)} %get-tuple-element.179.v_ref, bf16[192,512]{1,0:T(8,128)(2,1)} %get-tuple-element.287.rest_0_, bf16[192,512]{1,0:T(8,128)(2,1)} %copy-done.5, ...), custom_call_target="tpu_custom_call" | custom-call | flops 1811939328 | bytes 8388608 | tf_op jit(solution)/shard_map/norm1_grad/pallas_call | solution.py:363
  349.6 13.0 %collective-permute-done.44 = f32[100,256]{1,0:T(8,128)S(1)} collective-permute-done((f32[100,256]{1,0:T(8,128)S(1)}, f32[100,256]{1,0:T(8,128)S(1)}, u32[]{:S(2)}, u32[]{:S(2)}) %collective-permute-start.44) | collective-permute-done | bytes 102432 | tf_op jit(solution)/shard_map/ppermute | solution.py:716
  364.9 9.2 %collective-permute-done.52 = bf16[96,1728]{1,0:T(8,128)(2,1)S(1)} collective-permute-done((bf16[96,1728]{1,0:T(8,128)(2,1)}, bf16[96,1728]{1,0:T(8,128)(2,1)S(1)}, u32[]{:S(2)}, u32[]{:S(2)}) %collective-permute-start.52) | collective-permute-done | bytes 331808 | tf_op jit(solution)/shard_map/ppermute | solution.py:716
  382.5 5.0 %copied.1 = bf16[2048,768]{1,0:T(8,128)(2,1)} custom-call(s32[3]{0:T(128)} %add_add_fusion.1.sc_ref, bf16[2048,768]{1,0:T(8,128)(2,1)} %all-gather.20.cloned.1.call-done), custom_call_target="tpu_custom_call" | custom-call | bytes 4194304 | tf_op jit(solution)/shard_map/copied/pallas_call | solution.py:363
  391.5 3.3 collective-permute-done.50
  397.1 4.2 collective-permute-done.51
  401.5 28.7 %all-gather.12.cloned.1.call-done = bf16[2048,768]{1,0:T(8,128)(2,1)} async-done(((bf16[512,768]{1,0:T(8,128)(2,1)}), bf16[2048,768]{1,0:T(8,128)(2,1)}) %all-gather.12.cloned.1.call-update) | async-done | bytes 3145744 | tf_op jit(solution)/shard_map/all_gather | solution.py:903
  430.2 5.1 %bitcast_convert_fusion = f32[1,2048,768]{2,1,0:T(8,128)} fusion(bf16[2048,768]{1,0:T(8,128)(2,1)} %all-gather.12.cloned.1.call-done), kind=kLoop, calls=%fused_computation.2 | loop fusion | flops 1572864 | bytes 9437184 | tf_op jit(solution)/shard_map/reshape | solution.py:943
  (254 shorter events, 99.1 us)
Async XLA Ops:
  7.2 59.0 %all-gather.14.cloned.1.call-start = ((), (), s32[]{:S(2)}) async-start(), calls=%async_computation.3 | async-start | bytes 1474560 | tf_op jit(solution)/shard_map/all_gather | solution.py:784
  7.9 81.9 %all-gather.16.cloned.1.call-start = ((), (), s32[]{:S(2)}) async-start(), calls=%async_computation.4 | async-start | bytes 1474560 | tf_op jit(solution)/shard_map/all_gather | solution.py:785
  17.8 165.2 %all-gather.18.cloned.1.call-start = ((), (), s32[]{:S(2)}) async-start(), calls=%async_computation.5 | async-start | bytes 2088960 | tf_op jit(solution)/shard_map/all_gather | solution.py:725
  27.8 38.3 %collective-permute-start.6 = (bf16[2,208,192]{2,1,0:T(8,128)(2,1)S(1)}, bf16[2,208,192]{2,1,0:T(8,128)(2,1)S(1)}, u32[]{:S(2)}, u32[]{:S(2)}) collective-permute-start(bf16[2,208,192]{2,1,0:T(8,128)(2,1)S(1)} %pad_maximum_fusion.3), channel_id=1, source_target_pairs={{0,2},{1,3},{2,0},{3,1},{4,6},{5,7},{6,4},{7,5},{8,10},{9,11},{10,... | collective-permute-start | bytes 479240 | tf_op jit(solution)/shard_map/ppermute | solution.py:716
  39.4 29.0 %collective-permute-start.4 = (bf16[128,2048]{1,0:T(8,128)(2,1)}, bf16[128,2048]{1,0:T(8,128)(2,1)S(1)}, u32[]{:S(2)}, u32[]{:S(2)}) collective-permute-start(bf16[128,2048]{1,0:T(8,128)(2,1)} %get-tuple-element.182.rest_0_), channel_id=1, source_target_pairs={{0,4},{4,0},{1,5},{5,1},{2,6},{6,2},{3,7},{7,3},{8,12},{12,8},{9,1... | collective-permute-start | bytes 1572872 | tf_op jit(solution)/shard_map/ppermute | solution.py:711
  40.9 27.5 %collective-permute-start.5 = (bf16[128,2048]{1,0:T(8,128)(2,1)}, bf16[128,2048]{1,0:T(8,128)(2,1)S(1)}, u32[]{:S(2)}, u32[]{:S(2)}) collective-permute-start(bf16[128,2048]{1,0:T(8,128)(2,1)} %get-tuple-element.183.rest_1_.rest_0_), channel_id=1, source_target_pairs={{0,4},{4,0},{1,5},{5,1},{2,6},{6,2},{3,7},{7,3},{8,12},{12,8},{9,1... | collective-permute-start | bytes 1572872 | tf_op jit(solution)/shard_map/ppermute | solution.py:711
  41.4 48.4 %collective-permute-start.8 = (bf16[128,2048]{1,0:T(8,128)(2,1)}, bf16[128,2048]{1,0:T(8,128)(2,1)S(1)}, u32[]{:S(2)}, u32[]{:S(2)}) collective-permute-start(bf16[128,2048]{1,0:T(8,128)(2,1)} %get-tuple-element.184.rest_2_.rest_0_), channel_id=1, source_target_pairs={{0,4},{4,0},{1,5},{5,1},{2,6},{6,2},{3,7},{7,3},{8,12},{12,8},{9,1... | collective-permute-start | bytes 1572872 | tf_op jit(solution)/shard_map/ppermute | solution.py:711
  66.3 23.6 %collective-permute-start.7 = (bf16[4,208,192]{2,1,0:T(8,128)(2,1)S(1)}, bf16[4,208,192]{2,1,0:T(8,128)(2,1)S(1)}, u32[]{:S(2)}, u32[]{:S(2)}) collective-permute-start(bf16[4,208,192]{2,1,0:T(8,128)(2,1)S(1)} %pad_maximum_fusion.2.rest_8_), channel_id=1, source_target_pairs={{0,16},{8,24},{16,0},{24,8},{1,17},{9,25},{17,1},{25,9},{2,18},{10... | collective-permute-start | bytes 958472 | tf_op jit(solution)/shard_map/ppermute | solution.py:716
  67.8 47.5 %collective-permute-start.11 = (bf16[4,192,768]{2,1,0:T(8,128)(2,1)}, bf16[4,192,768]{2,1,0:T(8,128)(2,1)}, u32[]{:S(2)}, u32[]{:S(2)}) collective-permute-start(bf16[4,192,768]{2,1,0:T(8,128)(2,1)} %bitcast.122), channel_id=1, source_target_pairs={{0,16},{8,24},{16,0},{24,8},{1,17},{9,25},{17,1},{25,9},{2,18},{10... | collective-permute-start | bytes 3538952 | tf_op jit(solution)/shard_map/ppermute | solution.py:716
  90.6 37.6 %collective-permute-start.18 = (bf16[4,192,768]{2,1,0:T(8,128)(2,1)}, bf16[4,192,768]{2,1,0:T(8,128)(2,1)}, u32[]{:S(2)}, u32[]{:S(2)}) collective-permute-start(bf16[4,192,768]{2,1,0:T(8,128)(2,1)} %bitcast.125), channel_id=1, source_target_pairs={{0,16},{8,24},{16,0},{24,8},{1,17},{9,25},{17,1},{25,9},{2,18},{10... | collective-permute-start | bytes 3538952 | tf_op jit(solution)/shard_map/ppermute | solution.py:716
  128.9 134.2 %all-gather.20.cloned.1.call-start = ((), (), s32[]{:S(2)}) async-start(), calls=%async_computation.6 | async-start | bytes 3932160 | tf_op jit(solution)/shard_map/all_gather | solution.py:858
  160.6 22.4 %collective-permute-start.23 = (bf16[192,512]{1,0:T(8,128)(2,1)}, bf16[192,512]{1,0:T(8,128)(2,1)S(1)}, u32[]{:S(2)}, u32[]{:S(2)}) collective-permute-start(bf16[192,512]{1,0:T(8,128)(2,1)} %get-tuple-element.239), channel_id=1, source_target_pairs={{0,1},{1,0},{2,3},{3,2},{4,5},{5,4},{6,7},{7,6},{8,9},{9,8},{10,11... | collective-permute-start | bytes 589832 | tf_op jit(solution)/shard_map/ppermute | solution.py:716
  162.2 20.8 %collective-permute-start.24 = (bf16[192,512]{1,0:T(8,128)(2,1)}, bf16[192,512]{1,0:T(8,128)(2,1)S(1)}, u32[]{:S(2)}, u32[]{:S(2)}) collective-permute-start(bf16[192,512]{1,0:T(8,128)(2,1)} %get-tuple-element.240), channel_id=1, source_target_pairs={{0,2},{1,3},{2,0},{3,1},{4,6},{5,7},{6,4},{7,5},{8,10},{9,11},{10,... | collective-permute-start | bytes 589832 | tf_op jit(solution)/shard_map/ppermute | solution.py:716
  163.1 19.9 %collective-permute-start.25 = (bf16[192,512]{1,0:T(8,128)(2,1)}, bf16[192,512]{1,0:T(8,128)(2,1)S(1)}, u32[]{:S(2)}, u32[]{:S(2)}) collective-permute-start(bf16[192,512]{1,0:T(8,128)(2,1)} %get-tuple-element.241), channel_id=1, source_target_pairs={{0,3},{1,2},{2,1},{3,0},{4,7},{5,6},{6,5},{7,4},{8,11},{9,10},{10,... | collective-permute-start | bytes 589832 | tf_op jit(solution)/shard_map/ppermute | solution.py:716
  198.5 48.9 %collective-permute-start.30 = (bf16[1,128,2048]{2,1,0:T(8,128)(2,1)}, bf16[1,128,2048]{2,1,0:T(8,128)(2,1)}, u32[]{:S(2)}, u32[]{:S(2)}) collective-permute-start(bf16[1,128,2048]{2,1,0:T(8,128)(2,1)} %get-tuple-element.261), channel_id=1, source_target_pairs={{0,4},{4,0},{1,5},{5,1},{2,6},{6,2},{3,7},{7,3},{8,12},{12,8},{9,1... | collective-permute-start | bytes 1572872 | tf_op jit(solution)/shard_map/ppermute | solution.py:711
  199.0 141.0 %all-gather.22.cloned.1.call-start = ((), (), s32[]{:S(2)}) async-start(), calls=%async_computation.7 | async-start | bytes 2088960 | tf_op jit(solution)/shard_map/all_gather | solution.py:725
  206.4 36.7 %collective-permute-start.29 = (bf16[4,96,1728]{2,1,0:T(8,128)(2,1)}, bf16[4,96,1728]{2,1,0:T(8,128)(2,1)}, u32[]{:S(2)}, u32[]{:S(2)}) collective-permute-start(bf16[4,96,1728]{2,1,0:T(8,128)(2,1)} %dynamic-slice_bitcast_fusion), channel_id=1, source_target_pairs={{0,4},{4,0},{1,5},{5,1},{2,6},{6,2},{3,7},{7,3},{8,12},{12,8},{9,1... | collective-permute-start | bytes 3981320 | tf_op jit(solution)/shard_map/ppermute | solution.py:716
  207.9 35.2 %collective-permute-start.28 = (bf16[2,192,1728]{2,1,0:T(8,128)(2,1)S(1)}, bf16[2,192,1728]{2,1,0:T(8,128)(2,1)S(1)}, u32[]{:S(2)}, u32[]{:S(2)}) collective-permute-start(bf16[2,192,1728]{2,1,0:T(8,128)(2,1)S(1)} %get-tuple-element.367), channel_id=1, source_target_pairs={{0,16},{8,24},{16,0},{24,8},{1,17},{9,25},{17,1},{25,9},{2,18},{10... | collective-permute-start | bytes 3981320 | tf_op jit(solution)/shard_map/ppermute | solution.py:716
  238.5 31.6 %collective-permute-start.32 = (bf16[2,128,2048]{2,1,0:T(8,128)(2,1)}, bf16[2,128,2048]{2,1,0:T(8,128)(2,1)}, u32[]{:S(2)}, u32[]{:S(2)}) collective-permute-start(bf16[2,128,2048]{2,1,0:T(8,128)(2,1)} %get-tuple-element.265), channel_id=1, source_target_pairs={{0,4},{4,0},{1,5},{5,1},{2,6},{6,2},{3,7},{7,3},{8,12},{12,8},{9,1... | collective-permute-start | bytes 3145736 | tf_op jit(solution)/shard_map/ppermute | solution.py:711
  264.7 99.4 %reduce-scatter.2.cloned.1.call-start = ((), (), s32[]{:S(2)}) async-start(), calls=%async_computation.2 | async-start | bytes 1720320 | tf_op jit(solution)/shard_map/reduce_scatter | solution.py:887
  265.1 20.3 %collective-permute-start.33 = (bf16[2,96,1728]{2,1,0:T(8,128)(2,1)S(1)}, bf16[2,96,1728]{2,1,0:T(8,128)(2,1)S(1)}, u32[]{:S(2)}, u32[]{:S(2)}) collective-permute-start(bf16[2,96,1728]{2,1,0:T(8,128)(2,1)S(1)} %dynamic-slice_bitcast_fusion.1), channel_id=1, source_target_pairs={{0,4},{4,0},{1,5},{5,1},{2,6},{6,2},{3,7},{7,3},{8,12},{12,8},{9,1... | collective-permute-start | bytes 1990664 | tf_op jit(solution)/shard_map/ppermute | solution.py:716
  265.8 24.7 %collective-permute-start.34 = (bf16[192,512]{1,0:T(8,128)(2,1)}, bf16[192,512]{1,0:T(8,128)(2,1)S(1)}, u32[]{:S(2)}, u32[]{:S(2)}) collective-permute-start(bf16[192,512]{1,0:T(8,128)(2,1)} %get-tuple-element.270.rest_1_), channel_id=1, source_target_pairs={{0,1},{1,0},{2,3},{3,2},{4,5},{5,4},{6,7},{7,6},{8,9},{9,8},{10,11... | collective-permute-start | bytes 589832 | tf_op jit(solution)/shard_map/ppermute | solution.py:716
  266.8 26.2 %collective-permute-start.35 = (bf16[192,512]{1,0:T(8,128)(2,1)}, bf16[192,512]{1,0:T(8,128)(2,1)S(1)}, u32[]{:S(2)}, u32[]{:S(2)}) collective-permute-start(bf16[192,512]{1,0:T(8,128)(2,1)} %get-tuple-element.271.rest_2_), channel_id=1, source_target_pairs={{0,2},{1,3},{2,0},{3,1},{4,6},{5,7},{6,4},{7,5},{8,10},{9,11},{10,... | collective-permute-start | bytes 589832 | tf_op jit(solution)/shard_map/ppermute | solution.py:716
  268.2 24.8 %collective-permute-start.36 = (bf16[192,512]{1,0:T(8,128)(2,1)}, bf16[192,512]{1,0:T(8,128)(2,1)S(1)}, u32[]{:S(2)}, u32[]{:S(2)}) collective-permute-start(bf16[192,512]{1,0:T(8,128)(2,1)} %get-tuple-element.272.rest_3_), channel_id=1, source_target_pairs={{0,3},{1,2},{2,1},{3,0},{4,7},{5,6},{6,5},{7,4},{8,11},{9,10},{10,... | collective-permute-start | bytes 589832 | tf_op jit(solution)/shard_map/ppermute | solution.py:716
  285.4 23.1 %collective-permute-start.37 = (bf16[192,512]{1,0:T(8,128)(2,1)}, bf16[192,512]{1,0:T(8,128)(2,1)}, u32[]{:S(2)}, u32[]{:S(2)}) collective-permute-start(bf16[192,512]{1,0:T(8,128)(2,1)} %get-tuple-element.283.rest_5_), channel_id=1, source_target_pairs={{0,1},{1,0},{2,3},{3,2},{4,5},{5,4},{6,7},{7,6},{8,9},{9,8},{10,11... | collective-permute-start | bytes 589832 | tf_op jit(solution)/shard_map/ppermute | solution.py:716
  285.5 24.3 %collective-permute-start.38 = (bf16[192,512]{1,0:T(8,128)(2,1)}, bf16[192,512]{1,0:T(8,128)(2,1)}, u32[]{:S(2)}, u32[]{:S(2)}) collective-permute-start(bf16[192,512]{1,0:T(8,128)(2,1)} %get-tuple-element.284.rest_6_), channel_id=1, source_target_pairs={{0,2},{1,3},{2,0},{3,1},{4,6},{5,7},{6,4},{7,5},{8,10},{9,11},{10,... | collective-permute-start | bytes 589832 | tf_op jit(solution)/shard_map/ppermute | solution.py:716
  309.8 120.4 %all-gather.12.cloned.1.call-start = ((), (), s32[]{:S(2)}) async-start(), calls=%async_computation.1 | async-start | bytes 3932160 | tf_op jit(solution)/shard_map/all_gather | solution.py:903
  315.7 24.3 %collective-permute-start.41 = (bf16[192,512]{1,0:T(8,128)(2,1)}, bf16[192,512]{1,0:T(8,128)(2,1)S(1)}, u32[]{:S(2)}, u32[]{:S(2)}) collective-permute-start(bf16[192,512]{1,0:T(8,128)(2,1)} %get-tuple-element.300.rest_10_), channel_id=1, source_target_pairs={{0,2},{1,3},{2,0},{3,1},{4,6},{5,7},{6,4},{7,5},{8,10},{9,11},{10,... | collective-permute-start | bytes 589832 | tf_op jit(solution)/shard_map/ppermute | solution.py:716
  316.5 23.5 %collective-permute-start.42 = (bf16[192,512]{1,0:T(8,128)(2,1)}, bf16[192,512]{1,0:T(8,128)(2,1)S(1)}, u32[]{:S(2)}, u32[]{:S(2)}) collective-permute-start(bf16[192,512]{1,0:T(8,128)(2,1)} %get-tuple-element.301.rest_11_), channel_id=1, source_target_pairs={{0,3},{1,2},{2,1},{3,0},{4,7},{5,6},{6,5},{7,4},{8,11},{9,10},{10,... | collective-permute-start | bytes 589832 | tf_op jit(solution)/shard_map/ppermute | solution.py:716
  328.2 21.4 %collective-permute-start.43 = (f32[100,256]{1,0:T(8,128)S(1)}, f32[100,256]{1,0:T(8,128)S(1)}, u32[]{:S(2)}, u32[]{:S(2)}) collective-permute-start(f32[100,256]{1,0:T(8,128)S(1)} %concatenate.23), channel_id=1, source_target_pairs={{0,1},{1,0},{2,3},{3,2},{4,5},{5,4},{6,7},{7,6},{8,9},{9,8},{10,11... | collective-permute-start | bytes 307208 | tf_op jit(solution)/shard_map/ppermute | solution.py:716
  329.3 33.3 %collective-permute-start.44 = (f32[100,256]{1,0:T(8,128)S(1)}, f32[100,256]{1,0:T(8,128)S(1)}, u32[]{:S(2)}, u32[]{:S(2)}) collective-permute-start(f32[100,256]{1,0:T(8,128)S(1)} %concatenate.23), channel_id=1, source_target_pairs={{0,2},{1,3},{2,0},{3,1},{4,6},{5,7},{6,4},{7,5},{8,10},{9,11},{10,... | collective-permute-start | bytes 307208 | tf_op jit(solution)/shard_map/ppermute | solution.py:716
  331.0 31.6 %collective-permute-start.45 = (f32[100,256]{1,0:T(8,128)S(1)}, f32[100,256]{1,0:T(8,128)S(1)}, u32[]{:S(2)}, u32[]{:S(2)}) collective-permute-start(f32[100,256]{1,0:T(8,128)S(1)} %concatenate.23), channel_id=1, source_target_pairs={{0,3},{1,2},{2,1},{3,0},{4,7},{5,6},{6,5},{7,4},{8,11},{9,10},{10,... | collective-permute-start | bytes 307208 | tf_op jit(solution)/shard_map/ppermute | solution.py:716
  (64 other events, 708.1 us)
Sparse Core Ops, SparseCore 0:
  9.6 42.4 all-gather.13
  53.6 28.9 all-gather.15
  129.1 42.8 all-gather.17
  199.2 63.1 all-gather.19
  264.9 50.0 all-gather.21
  317.7 46.4 reduce-scatter.1
  365.8 64.3 all-gather.11
